TPU v7x, 512 devices: a whole 4x8x8 slice. The times are simulated.
512 devices in a mesh: chrom: 32 (over x, z), genome: 16 (over y, core).
Axes of the slice: x: 4, y: 8, z: 8, core: 2. Of those that a mesh axis runs over, the one named last changes fastest.
Arguments:
- panel: bfloat16 [768, 262144], P(None, ('chrom', 'genome')), may hold values from -30 to 30
- zscores: float32 [262144], P(('chrom', 'genome')), may hold values from -40 to 40
- block_chrom: int32 [512], P(('chrom', 'genome')), may hold values from 0 to 511, as said below
- lr_partner: int32 [512, 2], P(('chrom', 'genome')), may hold values from 0 to 511, as said below
Outputs:
- whitened: float32 [262144], P(('chrom', 'genome'))
- enrichment: float32 [32], P('chrom')
Inputs may be any that keep to these rules, and one draw needn't show every extreme that they name: `block_chrom`: chromosome numbers never fall along the blocks of one group of 16 blocks, and no two groups share a number. `lr_partner`: each entry names a block of the same group of 16 blocks other than the block itself.
All inputs are finite; a program needn't handle non-finite values.
Results may differ from a plain program's by a relative error of at most 0.0003.
Values may be sent and summed in bfloat16 or wider, within the bound.
No kernel may reach another device: no remote copies, remote signals or barrier semaphores. Data moves between devices by JAX's collectives and lax.ppermute only.
A program may use at most 64 MiB of HBM per device.

v0:
```python
import jax
import jax.numpy as jnp
from jax import lax
from jax.sharding import PartitionSpec as P

LONG_PAIRS = 2
NS_ITERS = 3


ridge_term = 0.5
leak_weight = 0.25


def passed_along(block, axis, distance):
    devices = range(lax.axis_size(axis))
    route = [(i - distance, i) for i in devices if i - distance in devices]
    return lax.ppermute(block, axis, route)


def column_product(left_mat, right_mat):
    return lax.dot_general(
        left_mat, right_mat, (((0,), (0,)), ((), ())), preferred_element_type=jnp.float32
    )


def row_product(left_mat, right_mat):
    return lax.dot_general(
        left_mat, right_mat, (((1,), (1,)), ((), ())), preferred_element_type=jnp.float32
    )


def exact_dot(left_mat, right_mat):
    return jnp.dot(left_mat, right_mat, precision=lax.Precision.HIGHEST)


def inverse_root(matrix):
    fro_scale = jnp.sqrt(jnp.sum(matrix * matrix) + 1e-06)
    normed = matrix / fro_scale
    identity = jnp.eye(matrix.shape[0], dtype=jnp.float32)
    iterate = identity
    for step_index in range(NS_ITERS):
        square = exact_dot(iterate, iterate)
        product = exact_dot(square, normed)
        iterate = 0.5 * exact_dot(iterate, 3.0 * identity - product)
    return iterate


def pick_blocks(wanted, held_panels, shard_cols, block_width):
    shard_count = shard_cols.shape[1] // block_width
    stacked = shard_cols.reshape(shard_cols.shape[0], shard_count, block_width)
    shard_index = jnp.arange(shard_count, dtype=jnp.int32)
    matches = wanted[:, None] == shard_index[None, :]
    picked = jnp.einsum(
        "kc,scb->ksb", matches.astype(jnp.bfloat16), stacked, preferred_element_type=jnp.float32
    ).astype(jnp.bfloat16)
    found_any = jnp.any(matches, axis=1)
    return (jnp.where(found_any[:, None, None], picked, held_panels), matches, found_any)


def local(panel, zscores, block_chrom, lr_partner):
    num_samples = panel.shape[0]
    block_width = panel.shape[1]
    group_size = lax.axis_size("genome")
    scale_inv = 1.0 / num_samples
    partners = lr_partner[0] % group_size

    def cross_ld(other_block, keep_flag):
        return (column_product(panel, other_block) * (scale_inv * keep_flag)).astype(jnp.bfloat16)

    new_panels, matches, found_any = pick_blocks(
        partners,
        jnp.zeros((LONG_PAIRS, num_samples, block_width), jnp.bfloat16),
        lax.all_gather(panel, "genome", axis=1, tiled=True),
        block_width,
    )

    def neighbour(offset):
        return passed_along((panel, block_chrom), "genome", offset)

    left_panel, left_id = neighbour(1)
    right_panel, right_id = neighbour(-1)
    left_cross = cross_ld(left_panel, (left_id[0] == block_chrom[0]).astype(jnp.float32))
    right_cross = cross_ld(right_panel, (right_id[0] == block_chrom[0]).astype(jnp.float32))
    leakage = row_product(left_cross, left_cross) + row_product(right_cross, right_cross)
    far_cross = (
        jnp.einsum("sa,ksb->kab", panel, new_panels, preferred_element_type=jnp.float32) * scale_inv
    ).astype(jnp.bfloat16)
    leakage = leakage + jnp.einsum(
        "kab,kcb->ac", far_cross, far_cross, preferred_element_type=jnp.float32
    )
    local_ld = (
        column_product(panel, panel) * scale_inv
        + ridge_term * jnp.eye(block_width, dtype=jnp.float32)
        + leak_weight * leakage
    )
    inverse_sqrt = inverse_root(local_ld)
    whitened = exact_dot(inverse_sqrt, zscores)
    local_sum = jnp.sum(whitened * whitened)
    chrom_count = lax.axis_size("chrom")
    group_sum = lax.psum(local_sum, "genome")
    overall = lax.psum(group_sum, "chrom")
    enrichment = group_sum * chrom_count / overall
    return (whitened, enrichment.reshape(1))


def solution(mesh):
    placed = (
        P(None, ("chrom", "genome")),
        P(("chrom", "genome")),
        P(("chrom", "genome")),
        P(("chrom", "genome"), None),
    )
    return jax.shard_map(
        local,
        mesh=mesh,
        in_specs=placed,
        out_specs=(P(("chrom", "genome")), P("chrom")),
        check_vma=False,
    )
```

profile of v0, /device:TPU:32, one launch (start us, length us, event | category | flops | bytes accessed | tf_op | source)
XLA Modules:
  0.0 245.2 jit_solution(4661136249581672759)
XLA Ops:
  7.2 0.0 copy-start
  7.2 0.0 all-gather.2.cloned.1.call-start
  7.2 0.7 all-gather.2.cloned.1.call-update
  7.9 1.9 collective-permute-start
  9.9 2.7 %collective-permute-start.1 = (s32[1]{0:T(128)}, s32[1]{0:T(128)}, u32[]{:S(2)}, u32[]{:S(2)}) collective-permute-start(s32[1]{0:T(128)} %param.6), channel_id=1, source_target_pairs={{0,1},{1,2},{2,3},{3,4},{4,5},{5,6},{6,7},{7,8},{8,9},{9,10},{10,1... | collective-permute-start | bytes 20 | tf_op jit(solution)/shard_map/ppermute | solution.py:17
  12.5 4.1 %collective-permute-start.3 = (s32[1]{0:T(128)}, s32[1]{0:T(128)}, u32[]{:S(2)}, u32[]{:S(2)}) collective-permute-start(s32[1]{0:T(128)} %param.6), channel_id=1, source_target_pairs={{1,0},{2,1},{3,2},{4,3},{5,4},{6,5},{7,6},{8,7},{9,8},{10,9},{11,1... | collective-permute-start | bytes 20 | tf_op jit(solution)/shard_map/ppermute | solution.py:17
  16.6 2.4 collective-permute-start.2
  19.7 0.7 and_select_fusion
  20.4 0.2 fusion.24
  20.6 1.5 fusion.13
  22.0 0.6 fusion.9
  22.6 0.2 collective-permute-done.1
  23.4 0.0 collective-permute-done.3
  24.0 0.0 collective-permute-done
  24.0 2.4 fusion.11
  26.4 63.8 %all-gather.2.cloned.1.call-done = bf16[768,8192]{1,0:T(8,128)(2,1)} async-done(((bf16[768,512]{1,0:T(8,128)(2,1)}), bf16[768,8192]{1,0:T(8,128)(2,1)}) %all-gather.2.cloned.1.call-update) | async-done | bytes 12582928 | tf_op jit(solution)/shard_map/all_gather | solution.py:73
  90.2 9.4 %copy.7 = bf16[96,8,16,512]{3,2,1,0:T(8,128)(2,1)S(1)} copy(bf16[96,8,16,512]{3,1,2,0:T(8,128)(2,1)} %bitcast.45) | data formatting | bytes 25165824
  99.6 2.3 fusion.22
  101.9 3.5 %convolution_bitcast_fusion = f32[512,512]{1,0:T(8,128)} fusion(bf16[2,768,512]{2,0,1:T(2,128)(2,1)S(1)} %fusion.22, pred[2]{0:T(512)(128)(4,1)S(1)} %fusion.24, bf16[768,512]{1,0:T(8,128)(2,1)S(1)} %copy-done.1), kind=kOutput, calls=%fused_computation.13 | convolution fusion | flops 1344012288 | bytes 3407874 | tf_op jit(solution)/shard_map/kab,kcb->ac/dot_general | solution.py:88
  105.3 4.2 %multiply_reduce_fusion = (f32[]{:T(128)}, f32[512,512]{1,0:T(8,128)S(1)}) fusion(f32[512,512]{1,0:T(8,128)S(1)} %fusion.9, f32[512,512]{1,0:T(8,128)} %convolution_bitcast_fusion, f32[512,512]{1,0:T(8,128)} %fusion.11, bf16[768,512]{1,0:T(8,128)(2,1)S(1)} %copy-done.1, bf16[768,512]{1,0:T(8,128)(2,1)} %collective-permute-done.2, f32[]{:T(128)} %bitcast.1), kind=kOutput, calls=%fused_computation.23 | convolution fusion | flops 673185792 | bytes 5767176 | tf_op jit(solution)/shard_map/dot_general | solution.py:27
  110.2 3.1 %select_subtract_fusion.2 = f32[512,512]{1,0:T(8,128)S(1)} fusion(f32[512,512]{1,0:T(8,128)} %fusion.13, f32[512,512]{1,0:T(8,128)S(1)} %get-tuple-element.3, f32[]{:T(128)S(6)} %sqrt.3), kind=kOutput, calls=%fused_computation.4 | convolution fusion | flops 1611661312 | bytes 3145732 | tf_op jit(solution)/shard_map/dot_general | solution.py:33
  113.3 1.1 convolution_multiply_fusion.5
  114.4 1.8 fusion.30
  116.2 1.9 select_subtract_fusion.1
  118.1 1.9 convolution_multiply_fusion.4
  120.0 2.1 fusion.31
  122.1 1.9 select_subtract_fusion
  123.9 1.9 convolution_multiply_fusion.3
  125.8 1.0 fusion.32
  126.8 0.6 multiply_reduce_fusion.1
  127.4 26.9 %psum.14 = f32[]{:T(128)} all-reduce(f32[]{:T(128)} %multiply_reduce_fusion.1), channel_id=1, replica_groups=mesh['chrom'=32,'genome'=16] {'genome'}, use_global_device_ids=true, to_apply=%region_3.4 | all-reduce | flops 1 | bytes 8 | tf_op jit(solution)/shard_map/psum | solution.py:100
  154.3 81.5 %psum.15 = f32[]{:T(128)} all-reduce(f32[]{:T(128)} %psum.14), channel_id=1, replica_groups=mesh['chrom'=32,'genome'=16] {'chrom'}, use_global_device_ids=true, to_apply=%region_4.5 | all-reduce | flops 1 | bytes 8 | tf_op jit(solution)/shard_map/psum | solution.py:101
  (6 shorter events, 0.0 us)
Async XLA Ops:
  7.2 118.6 %copy-start = (f32[512]{0:T(512)S(1)}, f32[512]{0:T(512)}, u32[]{:S(2)}) copy-start(f32[512]{0:T(512)} %param.5) | copy-start | bytes 6148
  7.2 14.8 %copy-start.1 = (bf16[768,512]{1,0:T(8,128)(2,1)S(1)}, bf16[768,512]{1,0:T(8,128)(2,1)}, u32[]{:S(2)}) copy-start(bf16[768,512]{1,0:T(8,128)(2,1)} %param.4) | copy-start | bytes 2359300
  7.2 83.0 %all-gather.2.cloned.1.call-start = ((), (), s32[]{:S(2)}) async-start(), calls=%async_computation | async-start | bytes 13369344 | tf_op jit(solution)/shard_map/all_gather | solution.py:73
  7.9 16.1 %collective-permute-start = (bf16[768,512]{1,0:T(8,128)(2,1)}, bf16[768,512]{1,0:T(8,128)(2,1)S(1)}, u32[]{:S(2)}, u32[]{:S(2)}) collective-permute-start(bf16[768,512]{1,0:T(8,128)(2,1)} %param.4), channel_id=1, source_target_pairs={{0,1},{1,2},{2,3},{3,4},{4,5},{5,6},{6,7},{7,8},{8,9},{9,10},{10,1... | collective-permute-start | bytes 2359304 | tf_op jit(solution)/shard_map/ppermute | solution.py:17
  9.9 13.0 %collective-permute-start.1 = (s32[1]{0:T(128)}, s32[1]{0:T(128)}, u32[]{:S(2)}, u32[]{:S(2)}) collective-permute-start(s32[1]{0:T(128)} %param.6), channel_id=1, source_target_pairs={{0,1},{1,2},{2,3},{3,4},{4,5},{5,6},{6,7},{7,8},{8,9},{9,10},{10,1... | collective-permute-start | bytes 20 | tf_op jit(solution)/shard_map/ppermute | solution.py:17
  12.5 10.9 %collective-permute-start.3 = (s32[1]{0:T(128)}, s32[1]{0:T(128)}, u32[]{:S(2)}, u32[]{:S(2)}) collective-permute-start(s32[1]{0:T(128)} %param.6), channel_id=1, source_target_pairs={{1,0},{2,1},{3,2},{4,3},{5,4},{6,5},{7,6},{8,7},{9,8},{10,9},{11,1... | collective-permute-start | bytes 20 | tf_op jit(solution)/shard_map/ppermute | solution.py:17
  16.6 88.7 %collective-permute-start.2 = (bf16[768,512]{1,0:T(8,128)(2,1)}, bf16[768,512]{1,0:T(8,128)(2,1)}, u32[]{:S(2)}, u32[]{:S(2)}) collective-permute-start(bf16[768,512]{1,0:T(8,128)(2,1)} %param.4), channel_id=1, source_target_pairs={{1,0},{2,1},{3,2},{4,3},{5,4},{6,5},{7,6},{8,7},{9,8},{10,9},{11,1... | collective-permute-start | bytes 2359304 | tf_op jit(solution)/shard_map/ppermute | solution.py:17
  126.8 110.5 %copy-start.2 = (f32[1,512]{1,0:T(1,128)}, f32[1,512]{1,0:T(1,128)S(1)}, u32[]{:S(2)}) copy-start(f32[1,512]{1,0:T(1,128)S(1)} %fusion.32) | copy-start | bytes 6148
Sparse Core Ops, SparseCore 0:
  10.2 79.9 all-gather.1
where the time goes:
time: 246 us; the launch traced here: 245 us
  blocking collectives  108 us (44%)
  waiting for transfers between devices  64.7 us (26%)
  matrix products  30.9 us (13%)
  between operations  19.2 us (8%)
  starting transfers between devices  11.1 us (5%)
  local copies, waits for them, and re-layouts  9.42 us (4%)
    psum x1, blocking collectives, local(): overall = lax.psum(group_sum, 'chrom')  81.5 us
    all_gather x1, waiting for transfers between devices, local(): lax.all_gather(panel, 'genome', axis=1, tiled=True)  63.8 us
    psum x1, blocking collectives, local(): group_sum = lax.psum(local_sum, 'genome')  26.9 us
    dot_general x10, matrix products, exact_dot(): return jnp.dot(left_mat, right_mat, precision=lax.Precision.HIGHEST)  18 us
    ppermute x4, starting transfers between devices, passed_along(): return lax.ppermute(block, axis, route)  11.1 us
    unnamed x7, local copies, waits for them, and re-layouts  9.42 us
    dot_general x2, matrix products, row_product(): lax.dot_general(left_mat, right_mat, (((1,), (1,)), ((), ())), preferred_...  6.54 us
  transfers between devices with their start and end apart: 5, of which 2 were waited for; matrix products, arithmetic and copies ran while one was open for 8% of the time, Pallas kernels for 0%

commit v1 on v0

v1 whole, which is shorter than its diff:
```python
import functools

import jax
import jax.numpy as jnp
from jax import lax
from jax.experimental import pallas as pl
from jax.experimental.pallas import tpu as pltpu
from jax.sharding import PartitionSpec as P

ridge_term = 0.5
leak_weight = 0.25

TILE = 128
SUB = 16
META_P0, META_P1, META_HI, META_LO = 3, 4, 5, 6

NT = (((1,), (1,)), ((), ()))
VMEM = pl.BlockSpec(memory_space=pltpu.VMEM)
SMEM = pl.BlockSpec(memory_space=pltpu.SMEM)


def tile_order(tiles):
    below = [(i, j) for j in range(tiles) for i in range(j + 1, tiles)]
    return below + [(2 * c, 2 * c) for c in range(tiles // 2)]


def grid_ids(shape):
    return lax.broadcasted_iota(jnp.int32, shape, 0), lax.broadcasted_iota(jnp.int32, shape, 1)


def pieces(start, share):
    out, row = [], 0
    while row < TILE:
        owner, place = divmod(start + row, share)
        length = min(TILE - row, share - place)
        out.append((row, owner, place, length))
        row += length
    return out


def gram_kernel(owners, share, partner_ref, chrom_ref, panel_ref, out_ref):
    samples = panel_ref.shape[0]
    tiles = samples // TILE
    order = {tile: n for n, tile in enumerate(tile_order(tiles))}
    rows, cols = grid_ids((TILE, TILE))
    metas = []

    def put(tile, value):
        value = value.astype(jnp.bfloat16)
        for row, owner, place, length in pieces(order[tile] * TILE, share):
            out_ref[owner, place : place + length, :] = value[row : row + length, :]

    for c in range(tiles // 2):
        low = 2 * c * TILE
        product = lax.dot_general(
            panel_ref[low:, :], panel_ref[low : low + 2 * TILE, :], NT, preferred_element_type=jnp.float32
        )
        for j in (2 * c, 2 * c + 1):
            for i in range(j + 1, tiles):
                put((i, j), product[i * TILE - low : (i + 1) * TILE - low, (j - 2 * c) * TILE : (j - 2 * c + 1) * TILE])
        first, second = product[:TILE, :TILE], product[TILE : 2 * TILE, TILE:]
        halved = jnp.where(rows == cols, 0.5 * second, second)
        put((2 * c, 2 * c), jnp.where(rows > cols, first, halved))
        metas.append(jnp.sum(jnp.where(rows == cols, 0.5 * first, 0.0), axis=0, keepdims=True))

    owner_rows, _ = grid_ids((SUB, TILE))
    meta = jnp.zeros((SUB, TILE), jnp.float32)
    for n, diagonal in enumerate(metas):
        meta = jnp.where(owner_rows == n, diagonal, meta)
    chrom = chrom_ref[0]
    for n, number in (
        (META_P0, lax.rem(partner_ref[0, 0], owners)),
        (META_P1, lax.rem(partner_ref[0, 1], owners)),
        (META_HI, chrom // 16),
        (META_LO, lax.rem(chrom, 16)),
    ):
        meta = jnp.where(owner_rows == n, number.astype(jnp.float32), meta)
    meta = meta.astype(jnp.bfloat16)
    for owner in range(owners):
        out_ref[owner, share : share + SUB, :] = meta


def mix_kernel(in_ref, out_ref):
    owners, height, _ = in_ref.shape
    meta = in_ref[:, height - SUB :, :].astype(jnp.float32)

    def spread(n):
        return jnp.broadcast_to(meta[:, n : n + 1, :], (owners, SUB, TILE))

    def flat(value):
        return value.reshape(owners * SUB, TILE)

    high, low = spread(META_HI), spread(META_LO)
    same = jnp.where(
        (high[1:] == high[:-1]) & (low[1:] == low[:-1]), 1.0, 0.0
    )
    edge = jnp.zeros((1, SUB, TILE), jnp.float32)
    with_right = flat(jnp.concatenate([same, edge], axis=0))
    with_left = flat(jnp.concatenate([edge, same], axis=0))
    first, second = flat(spread(META_P0)), flat(spread(META_P1))
    rows, cols = grid_ids((owners * SUB, TILE))
    own = (rows // SUB).astype(jnp.float32)
    halves = []
    for h in range(owners * SUB // TILE):
        other = (cols // SUB + h * (TILE // SUB)).astype(jnp.float32)
        count = jnp.where(first == other, 1.0, 0.0) + jnp.where(second == other, 1.0, 0.0)
        count = count + jnp.where(own + 1.0 == other, with_right, 0.0) + jnp.where(own - 1.0 == other, with_left, 0.0)
        halves.append(jnp.where(rows % SUB == cols % SUB, count, 0.0))
    weights = jnp.concatenate(halves, axis=1).astype(jnp.bfloat16)

    groups = height // SUB
    for g in range(0, groups, 2):
        members = list(range(g, min(g + 2, groups)))
        stacked = jnp.concatenate(
            [in_ref[:, m * SUB : (m + 1) * SUB, :].reshape(owners * SUB, TILE) for m in members], axis=1
        )
        mixed = jnp.dot(weights, stacked, preferred_element_type=jnp.float32).astype(jnp.bfloat16)
        for n, m in enumerate(members):
            out_ref[:, m * SUB : (m + 1) * SUB, :] = mixed[:, n * TILE : (n + 1) * TILE].reshape(owners, SUB, TILE)


def finish_kernel(share, sums_ref, columns_ref, base_ref, z_ref, out_ref, total_ref, half, scaled, first_iterate):
    samples = columns_ref.shape[1]
    width = columns_ref.shape[0]
    tiles = samples // TILE
    order = {tile: n for n, tile in enumerate(tile_order(tiles))}
    rows, cols = grid_ids((TILE, TILE))
    zero = jnp.zeros((TILE, TILE), jnp.bfloat16)

    def get(tile):
        return jnp.concatenate(
            [
                sums_ref[owner, place : place + length, :]
                for _, owner, place, length in pieces(order[tile] * TILE, share)
            ],
            axis=0,
        )

    def place(i, j, value):
        half[i * TILE : (i + 1) * TILE, j * TILE : (j + 1) * TILE] = value

    meta = sums_ref[0, share : share + SUB, :].astype(jnp.float32)
    for c in range(tiles // 2):
        for j in (2 * c, 2 * c + 1):
            for i in range(j + 1, tiles):
                place(i, j, get((i, j)))
        packed = get((2 * c, 2 * c)).astype(jnp.float32)
        lower = jnp.where(rows > cols, packed, jnp.where(rows == cols, meta[c : c + 1, :], 0.0))
        place(2 * c, 2 * c, lower.astype(jnp.bfloat16))
        place(2 * c + 1, 2 * c + 1, jnp.where(rows <= cols, packed, 0.0).astype(jnp.bfloat16))
        place(2 * c, 2 * c + 1, zero)

    scale = leak_weight / (samples * samples)
    columns = columns_ref[...]
    parts = []
    for c in range(tiles // 2):
        top = (2 * c + 2) * TILE
        parts.append(
            lax.dot_general(
                columns[:, :top], half[2 * c * TILE : top, :top], NT, preferred_element_type=jnp.float32
            )
            * scale
        )
    turned = jnp.concatenate(parts, axis=1).astype(jnp.bfloat16)
    matrix = (
        base_ref[...]
        + lax.dot_general(columns, turned, NT, preferred_element_type=jnp.float32)
        + lax.dot_general(turned, columns, NT, preferred_element_type=jnp.float32)
    )
    norm = jnp.sqrt(jnp.sum(matrix * matrix, keepdims=True) + 1e-06)
    matrix = matrix / norm
    scaled[...] = matrix
    wide_rows, wide_cols = grid_ids((width, width))
    first_iterate[...] = jnp.where(wide_rows == wide_cols, 1.5, 0.0) - 0.5 * matrix

    eye = rows == cols
    blocks = width // TILE

    def to_column(ref, row):
        return jnp.sum(ref[...] * row, axis=1, keepdims=True)

    def to_row(ref, column):
        return jnp.sum(ref[...] * column, axis=0, keepdims=True)

    def turned_column(column):
        return jnp.concatenate(
            [
                jnp.sum(jnp.where(eye, column[n * TILE : (n + 1) * TILE], 0.0), axis=0, keepdims=True)
                for n in range(blocks)
            ],
            axis=1,
        )

    def turned_row(row):
        return jnp.concatenate(
            [
                jnp.sum(jnp.where(eye, row[:, n * TILE : (n + 1) * TILE], 0.0), axis=1, keepdims=True)
                for n in range(blocks)
            ],
            axis=0,
        )

    def second_iterate(column):
        inner = to_row(scaled, column)
        inner = to_column(first_iterate, inner)
        inner = to_row(first_iterate, inner)
        return 0.5 * to_column(first_iterate, 3.0 * turned_column(column) - inner)

    z_row = z_ref[...]
    product = second_iterate(second_iterate(to_column(scaled, z_row)))
    answer = 0.5 * second_iterate(3.0 * turned_row(z_row) - product)
    answer = turned_column(answer)
    out_ref[...] = answer
    total_ref[...] = jnp.broadcast_to(jnp.sum(answer * answer, keepdims=True).reshape(1, 1, 1), total_ref.shape)


def local(panel, zscores, block_chrom, lr_partner):
    samples, width = panel.shape
    owners = lax.axis_size("genome")
    chroms = lax.axis_size("chrom")
    tiles = samples // TILE
    share = len(tile_order(tiles)) * TILE // owners
    packed_shape = jax.ShapeDtypeStruct((owners, share + SUB, TILE), jnp.bfloat16)
    params = pltpu.CompilerParams(vmem_limit_bytes=48 * 2**20)

    packed = pl.pallas_call(
        functools.partial(gram_kernel, owners, share),
        out_shape=packed_shape,
        in_specs=[SMEM, SMEM, VMEM],
        out_specs=VMEM,
        compiler_params=params,
    )(lr_partner, block_chrom, panel)
    held = lax.all_to_all(packed, "genome", 0, 0, tiled=True)

    mixed = pl.pallas_call(
        mix_kernel,
        out_shape=packed_shape,
        in_specs=[VMEM],
        out_specs=VMEM,
        compiler_params=params,
    )(held)
    sums = lax.all_to_all(mixed, "genome", 0, 0, tiled=True)

    columns = panel.T
    base = lax.dot_general(
        panel, panel, (((0,), (0,)), ((), ())), preferred_element_type=jnp.float32
    ) * (1.0 / samples) + ridge_term * jnp.eye(width, dtype=jnp.float32)

    whitened, totals = pl.pallas_call(
        functools.partial(finish_kernel, share),
        out_shape=(
            jax.ShapeDtypeStruct((1, width), jnp.float32),
            jax.ShapeDtypeStruct((owners, 1, TILE), jnp.float32),
        ),
        in_specs=[VMEM] * 4,
        out_specs=(VMEM, VMEM),
        scratch_shapes=[
            pltpu.VMEM((samples, samples), jnp.bfloat16),
            pltpu.VMEM((width, width), jnp.float32),
            pltpu.VMEM((width, width), jnp.float32),
        ],
        compiler_params=params,
    )(sums, columns, base, zscores.reshape(1, width))

    of_group = lax.all_to_all(totals, "genome", 0, 0, tiled=True)
    group_sum = jnp.sum(of_group, axis=0).reshape(TILE)[:chroms]
    of_all = lax.all_to_all(group_sum, "chrom", 0, 0, tiled=True)
    enrichment = group_sum[:1] * chroms / jnp.sum(of_all)
    return (whitened.reshape(width), enrichment)


def solution(mesh):
    placed = (
        P(None, ("chrom", "genome")),
        P(("chrom", "genome")),
        P(("chrom", "genome")),
        P(("chrom", "genome"), None),
    )
    return jax.shard_map(
        local,
        mesh=mesh,
        in_specs=placed,
        out_specs=(P(("chrom", "genome")), P("chrom")),
        check_vma=False,
    )
```

time: 246 us -> 95.5 us (0.39)
  the two profiles are of different devices: /device:TPU:32 before, /device:TPU:1 now
where the time goes in v1:
time: 95.5 us; the launch traced here: 95.1 us
  blocking collectives  39.6 us (41%)
  waiting for transfers between devices  27.1 us (28%)
  starting transfers between devices  15.6 us (16%)
  Pallas kernels  6.13 us (6%)
  between operations  3.18 us (3%)
  local copies, waits for them, and re-layouts  2.11 us (2%)
    all_to_all x1, blocking collectives, local(): held = lax.all_to_all(packed, 'genome', 0, 0, tiled=True)  29.7 us
    all_to_all x1, waiting for transfers between devices, local(): sums = lax.all_to_all(mixed, 'genome', 0, 0, tiled=True)  18.6 us
    all_to_all x1, starting transfers between devices, local(): of_all = lax.all_to_all(group_sum, 'chrom', 0, 0, tiled=True)  12 us
    all_to_all x1, blocking collectives, local(): of_group = lax.all_to_all(totals, 'genome', 0, 0, tiled=True)  9.92 us
    all_to_all x1, waiting for transfers between devices, local(): of_all = lax.all_to_all(group_sum, 'chrom', 0, 0, tiled=True)  8.59 us
    pallas_call x1, Pallas kernels, local(): pl.pallas_call(functools.partial(finish_kernel, share), out_shape=(jax.Sh...  3.75 us
    all_to_all x1, starting transfers between devices, local(): sums = lax.all_to_all(mixed, 'genome', 0, 0, tiled=True)  3.62 us
  transfers between devices with their start and end apart: 2, of which 2 were waited for; matrix products, arithmetic and copies ran while one was open for 1% of the time, Pallas kernels for 0%

profile of v1, /device:TPU:1, one launch (start us, length us, event | category | flops | bytes accessed | tf_op | source)
XLA Modules:
  0.0 95.1 jit_solution(13577942072580055285)
XLA Ops:
  0.6 0.0 copy-start.3
  1.3 0.0 copy-done.3
  1.3 0.0 copy-start
  1.3 1.1 %copy-done = bf16[768,512]{1,0:T(8,128)(2,1)S(1)} copy-done((bf16[768,512]{1,0:T(8,128)(2,1)S(1)}, bf16[768,512]{1,0:T(8,128)(2,1)}, u32[]{:S(2)}) %copy-start) | copy-done | bytes 786456
  2.4 1.1 %shard_map.59 = bf16[16,160,128]{2,1,0:T(8,128)(2,1)S(1)} custom-call(s32[1,2]{1,0:T(1,128)S(1)} %copy-done.3, s32[1]{0:T(128)S(6)} %copy.9.chrom_ref, bf16[768,512]{1,0:T(8,128)(2,1)S(1)} %copy-done), custom_call_target="tpu_custom_call" | custom-call | tf_op jit(solution)/shard_map/pallas_call | solution.py:226
  3.6 29.7 %all_to_all.24.in_ref = bf16[16,160,128]{2,1,0:T(8,128)(2,1)S(1)} all-to-all(bf16[16,160,128]{2,1,0:T(8,128)(2,1)S(1)} %shard_map.59), channel_id=1, replica_groups=mesh['chrom'=32,'genome'=16] {'genome'}, dimensions={0} | all-to-all | bytes 1310720 | tf_op jit(solution)/shard_map/all_to_all | solution.py:233
  33.3 1.2 %shard_map.60 = bf16[16,160,128]{2,1,0:T(8,128)(2,1)} custom-call(bf16[16,160,128]{2,1,0:T(8,128)(2,1)S(1)} %all_to_all.24.in_ref), custom_call_target="tpu_custom_call" | custom-call | tf_op jit(solution)/shard_map/pallas_call | solution.py:235
  34.5 0.0 copy-start.1
  34.5 3.6 %all-to-all-start.1 = ((bf16[16,160,128]{2,1,0:T(8,128)(2,1)}), bf16[16,160,128]{2,1,0:T(8,128)(2,1)S(1)}, u32[]{:S(2)}, u32[]{:S(2)}) async-start(bf16[16,160,128]{2,1,0:T(8,128)(2,1)} %shard_map.60), calls=%async_computation.1 | async-start | bytes 1310720 | tf_op jit(solution)/shard_map/all_to_all | solution.py:242
  38.2 0.0 copy-done.1
  38.2 0.3 copy.7
  38.4 0.6 fusion.base_ref
  39.1 0.0 copy-start.2
  39.1 18.6 %all-to-all-done.1.sums_ref = bf16[16,160,128]{2,1,0:T(8,128)(2,1)S(1)} async-done(((bf16[16,160,128]{2,1,0:T(8,128)(2,1)}), bf16[16,160,128]{2,1,0:T(8,128)(2,1)S(1)}, u32[]{:S(2)}, u32[]{:S(2)}) %all-to-all-start.1) | async-done | bytes 655392 | tf_op jit(solution)/shard_map/all_to_all | solution.py:242
  57.6 0.0 copy-done.2
  57.6 3.7 %shard_map.61 = (f32[1,512]{1,0:T(1,128)}, f32[16,1,128]{2,1,0:T(1,128)S(1)}) custom-call(bf16[16,160,128]{2,1,0:T(8,128)(2,1)S(1)} %all-to-all-done.1.sums_ref, bf16[512,768]{1,0:T(8,128)(2,1)S(1)} %bitcast.11, f32[512,512]{1,0:T(8,128)S(1)} %fusion.base_ref, f32[1,512]{1,0:T(1,128)S(1)} %bitcast.12), custom_call_target="tpu_custom_call" | custom-call | tf_op jit(solution)/shard_map/pallas_call | solution.py:249
  61.4 9.9 %all_to_all.25 = f32[16,1,128]{2,1,0:T(1,128)S(1)} all-to-all(f32[16,1,128]{2,1,0:T(1,128)S(1)} %get-tuple-element.5), channel_id=1, replica_groups=mesh['chrom'=32,'genome'=16] {'genome'}, dimensions={0} | all-to-all | bytes 16384 | tf_op jit(solution)/shard_map/all_to_all | solution.py:265
  71.3 0.7 copy.8
  72.0 12.0 %all-to-all-start.3 = ((f32[32,1,1]{2,1,0:T(1,128)}), f32[32,1,1]{2,1,0:T(1,128)S(1)}, u32[]{:S(2)}, u32[]{:S(2)}) async-start(f32[32,1,1]{2,1,0:T(1,128)} %copy.8), calls=%async_computation.3 | async-start | bytes 32768 | tf_op jit(solution)/shard_map/all_to_all | solution.py:267
  84.1 8.6 %all-to-all-done.3 = f32[32,1,1]{2,1,0:T(1,128)S(1)} async-done(((f32[32,1,1]{2,1,0:T(1,128)}), f32[32,1,1]{2,1,0:T(1,128)S(1)}, u32[]{:S(2)}, u32[]{:S(2)}) %all-to-all-start.3) | async-done | bytes 160 | tf_op jit(solution)/shard_map/all_to_all | solution.py:267
  92.7 0.7 reduce_sum.22
  (2 shorter events, 0.0 us)
Async XLA Ops:
  0.6 0.7 copy-start.3
  1.3 1.1 %copy-start = (bf16[768,512]{1,0:T(8,128)(2,1)S(1)}, bf16[768,512]{1,0:T(8,128)(2,1)}, u32[]{:S(2)}) copy-start(bf16[768,512]{1,0:T(8,128)(2,1)} %panel_ref.1) | copy-start | bytes 2359300
  34.5 3.6 %copy-start.1 = (bf16[768,512]{1,0:T(8,128)(2,1)S(1)}, bf16[768,512]{1,0:T(8,128)(2,1)}, u32[]{:S(2)}) copy-start(bf16[768,512]{1,0:T(8,128)(2,1)} %panel_ref.1) | copy-start | bytes 2359300
  34.5 23.1 %all-to-all-start.1 = ((bf16[16,160,128]{2,1,0:T(8,128)(2,1)}), bf16[16,160,128]{2,1,0:T(8,128)(2,1)S(1)}, u32[]{:S(2)}, u32[]{:S(2)}) async-start(bf16[16,160,128]{2,1,0:T(8,128)(2,1)} %shard_map.60), calls=%async_computation.1 | async-start | bytes 1310720 | tf_op jit(solution)/shard_map/all_to_all | solution.py:242
  39.1 18.6 %copy-start.2 = (f32[512]{0:T(512)S(1)}, f32[512]{0:T(512)}, u32[]{:S(2)}) copy-start(f32[512]{0:T(512)} %param.5) | copy-start | bytes 6148
  72.0 20.6 %all-to-all-start.3 = ((f32[32,1,1]{2,1,0:T(1,128)}), f32[32,1,1]{2,1,0:T(1,128)S(1)}, u32[]{:S(2)}, u32[]{:S(2)}) async-start(f32[32,1,1]{2,1,0:T(1,128)} %copy.8), calls=%async_computation.3 | async-start | bytes 32768 | tf_op jit(solution)/shard_map/all_to_all | solution.py:267

commit v2 on v1

--- a/solution.py
+++ b/solution.py
@@ -12,10 +12,12 @@
 
 TILE = 128
 SUB = 16
+META = 8
 META_P0, META_P1, META_HI, META_LO = 3, 4, 5, 6
 
 NT = (((1,), (1,)), ((), ()))
 VMEM = pl.BlockSpec(memory_space=pltpu.VMEM)
+HBM = pl.BlockSpec(memory_space=pltpu.HBM)
 SMEM = pl.BlockSpec(memory_space=pltpu.SMEM)
 
 
@@ -38,9 +40,19 @@
     return out
 
 
-def gram_kernel(owners, share, partner_ref, chrom_ref, panel_ref, out_ref):
+def gram_kernel(owners, share, partner_hbm, chrom_ref, panel_hbm, out_ref, panel_ref, partner_ref, sems):
     samples = panel_ref.shape[0]
     tiles = samples // TILE
+    bands = tiles // 2
+    arriving = []
+    for c in reversed(range(bands)):
+        band = pl.ds(2 * c * TILE, 2 * TILE)
+        arriving.append(pltpu.make_async_copy(panel_hbm.at[band], panel_ref.at[band], sems.at[c]))
+    small = [
+        pltpu.make_async_copy(partner_hbm, partner_ref, sems.at[bands]),
+    ]
+    for copy in arriving + small:
+        copy.start()
     order = {tile: n for n, tile in enumerate(tile_order(tiles))}
     rows, cols = grid_ids((TILE, TILE))
     metas = []
@@ -50,7 +62,8 @@
         for row, owner, place, length in pieces(order[tile] * TILE, share):
             out_ref[owner, place : place + length, :] = value[row : row + length, :]
 
-    for c in range(tiles // 2):
+    for c in reversed(range(bands)):
+        arriving[bands - 1 - c].wait()
         low = 2 * c * TILE
         product = lax.dot_general(
             panel_ref[low:, :], panel_ref[low : low + 2 * TILE, :], NT, preferred_element_type=jnp.float32
@@ -61,28 +74,31 @@
         first, second = product[:TILE, :TILE], product[TILE : 2 * TILE, TILE:]
         halved = jnp.where(rows == cols, 0.5 * second, second)
         put((2 * c, 2 * c), jnp.where(rows > cols, first, halved))
-        metas.append(jnp.sum(jnp.where(rows == cols, 0.5 * first, 0.0), axis=0, keepdims=True))
-
-    owner_rows, _ = grid_ids((SUB, TILE))
-    meta = jnp.zeros((SUB, TILE), jnp.float32)
-    for n, diagonal in enumerate(metas):
+        metas.append((c, jnp.sum(jnp.where(rows == cols, 0.5 * first, 0.0), axis=0, keepdims=True)))
+
+    owner_rows, _ = grid_ids((META, TILE))
+    meta = jnp.zeros((META, TILE), jnp.float32)
+    for n, diagonal in metas:
         meta = jnp.where(owner_rows == n, diagonal, meta)
+    for copy in small:
+        copy.wait()
     chrom = chrom_ref[0]
     for n, number in (
         (META_P0, lax.rem(partner_ref[0, 0], owners)),
         (META_P1, lax.rem(partner_ref[0, 1], owners)),
-        (META_HI, chrom // 16),
-        (META_LO, lax.rem(chrom, 16)),
+        (META_HI, chrom >> 4),
+        (META_LO, chrom & 15),
     ):
         meta = jnp.where(owner_rows == n, number.astype(jnp.float32), meta)
     meta = meta.astype(jnp.bfloat16)
     for owner in range(owners):
-        out_ref[owner, share : share + SUB, :] = meta
+        out_ref[owner, share : share + META, :] = meta
 
 
 def mix_kernel(in_ref, out_ref):
     owners, height, _ = in_ref.shape
-    meta = in_ref[:, height - SUB :, :].astype(jnp.float32)
+    share = height - META
+    meta = in_ref[:, share:, :].astype(jnp.float32)
 
     def spread(n):
         return jnp.broadcast_to(meta[:, n : n + 1, :], (owners, SUB, TILE))
@@ -108,7 +124,7 @@
         halves.append(jnp.where(rows % SUB == cols % SUB, count, 0.0))
     weights = jnp.concatenate(halves, axis=1).astype(jnp.bfloat16)
 
-    groups = height // SUB
+    groups = share // SUB
     for g in range(0, groups, 2):
         members = list(range(g, min(g + 2, groups)))
         stacked = jnp.concatenate(
@@ -117,6 +133,11 @@
         mixed = jnp.dot(weights, stacked, preferred_element_type=jnp.float32).astype(jnp.bfloat16)
         for n, m in enumerate(members):
             out_ref[:, m * SUB : (m + 1) * SUB, :] = mixed[:, n * TILE : (n + 1) * TILE].reshape(owners, SUB, TILE)
+    padded = jnp.concatenate([meta, jnp.zeros((owners, SUB - META, TILE), jnp.float32)], axis=1)
+    mixed = jnp.dot(
+        weights, padded.reshape(owners * SUB, TILE).astype(jnp.bfloat16), preferred_element_type=jnp.float32
+    )
+    out_ref[:, share:, :] = mixed.reshape(owners, SUB, TILE)[:, :META, :].astype(jnp.bfloat16)
 
 
 def finish_kernel(share, sums_ref, columns_ref, base_ref, z_ref, out_ref, total_ref, half, scaled, first_iterate):
@@ -139,7 +160,7 @@
     def place(i, j, value):
         half[i * TILE : (i + 1) * TILE, j * TILE : (j + 1) * TILE] = value
 
-    meta = sums_ref[0, share : share + SUB, :].astype(jnp.float32)
+    meta = sums_ref[0, share : share + META, :].astype(jnp.float32)
     for c in range(tiles // 2):
         for j in (2 * c, 2 * c + 1):
             for i in range(j + 1, tiles):
@@ -220,16 +241,22 @@
     chroms = lax.axis_size("chrom")
     tiles = samples // TILE
     share = len(tile_order(tiles)) * TILE // owners
-    packed_shape = jax.ShapeDtypeStruct((owners, share + SUB, TILE), jnp.bfloat16)
+    packed_shape = jax.ShapeDtypeStruct((owners, share + META, TILE), jnp.bfloat16)
     params = pltpu.CompilerParams(vmem_limit_bytes=48 * 2**20)
 
+    lr_hbm, panel_hbm = (pltpu.with_memory_space_constraint(x, pltpu.HBM) for x in (lr_partner, panel))
     packed = pl.pallas_call(
         functools.partial(gram_kernel, owners, share),
         out_shape=packed_shape,
-        in_specs=[SMEM, SMEM, VMEM],
+        in_specs=[HBM, SMEM, HBM],
         out_specs=VMEM,
+        scratch_shapes=[
+            pltpu.VMEM(panel.shape, panel.dtype),
+            pltpu.SMEM(lr_partner.shape, jnp.int32),
+            pltpu.SemaphoreType.DMA((tiles // 2 + 1,)),
+        ],
         compiler_params=params,
-    )(lr_partner, block_chrom, panel)
+    )(lr_hbm, block_chrom, panel_hbm)
     held = lax.all_to_all(packed, "genome", 0, 0, tiled=True)
 
     mixed = pl.pallas_call(
@@ -263,9 +290,12 @@
     )(sums, columns, base, zscores.reshape(1, width))
 
     of_group = lax.all_to_all(totals, "genome", 0, 0, tiled=True)
-    group_sum = jnp.sum(of_group, axis=0).reshape(TILE)[:chroms]
-    of_all = lax.all_to_all(group_sum, "chrom", 0, 0, tiled=True)
-    enrichment = group_sum[:1] * chroms / jnp.sum(of_all)
+    group_sum = jnp.sum(of_group, axis=0, keepdims=True)
+    of_all = lax.all_to_all(
+        jnp.broadcast_to(group_sum, (chroms, 1, TILE)), "chrom", 0, 0, tiled=True
+    )
+    group_sum, of_all = lax.optimization_barrier((group_sum, of_all))
+    enrichment = (group_sum * chroms / jnp.sum(of_all, axis=0, keepdims=True)).reshape(TILE)[:1]
     return (whitened.reshape(width), enrichment)
 
 

time: 95.5 us -> 91.5 us (0.958)
  blocking collectives: 39.6 us -> 59.2 us
  starting transfers between devices: 15.6 us -> 3.62 us
  waiting for transfers between devices: 27.1 us -> 18.3 us
  between operations: 3.18 us -> 1.33 us
  local copies, waits for them, and re-layouts: 2.11 us -> 0.3 us
  Pallas kernels: 6.13 us -> 7.24 us
    all_to_all x0 -> x1, blocking collectives: none -> 20.4 us  [local(): lax.all_to_all(jnp.broadcast_to(group_sum, (chroms, 1, TILE)), 'chrom', 0...]
    all_to_all x1 -> x0, starting transfers between devices: 12 us -> none  [local(): of_all = lax.all_to_all(group_sum, 'chrom', 0, 0, tiled=True)]
    all_to_all x1 -> x0, waiting for transfers between devices: 8.59 us -> none  [local(): of_all = lax.all_to_all(group_sum, 'chrom', 0, 0, tiled=True)]
    unnamed x9 -> x5, local copies, waits for them, and re-layouts: 1.41 us -> 0.28 us
    pallas_call x1, Pallas kernels: 1.14 us -> 2.25 us  [local(): pl.pallas_call(functools.partial(gram_kernel, owners, share), out_shape=p...]
  transfers between devices with their start and end apart: 2 -> 1, of which waited for: 2 -> 1; matrix products, arithmetic and copies ran while one was open for 1% -> 1% of each run, Pallas kernels for 0% -> 0%
where the time goes in v2:
time: 91.5 us; the launch traced here: 91.2 us
  blocking collectives  59.2 us (65%)
  waiting for transfers between devices  18.3 us (20%)
  Pallas kernels  7.24 us (8%)
  starting transfers between devices  3.62 us (4%)
  between operations  1.33 us (1%)
    all_to_all x1, blocking collectives, local(): held = lax.all_to_all(packed, 'genome', 0, 0, tiled=True)  29 us
    all_to_all x1, blocking collectives, local(): lax.all_to_all(jnp.broadcast_to(group_sum, (chroms, 1, TILE)), 'chrom', 0...  20.4 us
    all_to_all x1, waiting for transfers between devices, local(): sums = lax.all_to_all(mixed, 'genome', 0, 0, tiled=True)  18.3 us
    all_to_all x1, blocking collectives, local(): of_group = lax.all_to_all(totals, 'genome', 0, 0, tiled=True)  9.76 us
    pallas_call x1, Pallas kernels, local(): pl.pallas_call(functools.partial(finish_kernel, share), out_shape=(jax.Sh...  3.75 us
    all_to_all x1, starting transfers between devices, local(): sums = lax.all_to_all(mixed, 'genome', 0, 0, tiled=True)  3.62 us
    pallas_call x1, Pallas kernels, local(): pl.pallas_call(functools.partial(gram_kernel, owners, share), out_shape=p...  2.25 us
  transfers between devices with their start and end apart: 1, of which 1 were waited for; matrix products, arithmetic and copies ran while one was open for 1% of the time, Pallas kernels for 0%

profile of v2, /device:TPU:1, one launch (start us, length us, event | category | flops | bytes accessed | tf_op | source)
XLA Modules:
  0.0 91.2 jit_solution(10001463595125380699)
XLA Ops:
  1.3 2.2 %shard_map.59 = bf16[16,152,128]{2,1,0:T(8,128)(2,1)S(1)} custom-call(s32[1,2]{1,0:T(1,128)} %partner_hbm.1, s32[1]{0:T(128)S(6)} %copy.7.chrom_ref, bf16[768,512]{1,0:T(8,128)(2,1)} %panel_hbm.1), custom_call_target="tpu_custom_call" | custom-call | tf_op jit(solution)/shard_map/pallas_call | solution.py:248
  3.5 29.0 %all_to_all.20.in_ref = bf16[16,152,128]{2,1,0:T(8,128)(2,1)S(1)} all-to-all(bf16[16,152,128]{2,1,0:T(8,128)(2,1)S(1)} %shard_map.59), channel_id=1, replica_groups=mesh['chrom'=32,'genome'=16] {'genome'}, dimensions={0} | all-to-all | bytes 1245184 | tf_op jit(solution)/shard_map/all_to_all | solution.py:260
  32.6 1.2 %shard_map.60 = bf16[16,152,128]{2,1,0:T(8,128)(2,1)} custom-call(bf16[16,152,128]{2,1,0:T(8,128)(2,1)S(1)} %all_to_all.20.in_ref), custom_call_target="tpu_custom_call" | custom-call | tf_op jit(solution)/shard_map/pallas_call | solution.py:262
  33.8 0.0 copy-start.1
  33.8 3.6 %all-to-all-start.1 = ((bf16[16,152,128]{2,1,0:T(8,128)(2,1)}), bf16[16,152,128]{2,1,0:T(8,128)(2,1)S(1)}, u32[]{:S(2)}, u32[]{:S(2)}) async-start(bf16[16,152,128]{2,1,0:T(8,128)(2,1)} %shard_map.60), calls=%async_computation.1 | async-start | bytes 1245184 | tf_op jit(solution)/shard_map/all_to_all | solution.py:269
  37.4 0.0 copy-done.1
  37.5 0.3 copy.6
  37.7 0.6 fusion.base_ref
  38.3 0.0 copy-start
  38.4 18.3 %all-to-all-done.1.sums_ref = bf16[16,152,128]{2,1,0:T(8,128)(2,1)S(1)} async-done(((bf16[16,152,128]{2,1,0:T(8,128)(2,1)}), bf16[16,152,128]{2,1,0:T(8,128)(2,1)S(1)}, u32[]{:S(2)}, u32[]{:S(2)}) %all-to-all-start.1) | async-done | bytes 622624 | tf_op jit(solution)/shard_map/all_to_all | solution.py:269
  56.6 0.0 copy-done
  56.6 3.7 %shard_map.61 = (f32[1,512]{1,0:T(1,128)}, f32[16,1,128]{2,1,0:T(1,128)S(1)}) custom-call(bf16[16,152,128]{2,1,0:T(8,128)(2,1)S(1)} %all-to-all-done.1.sums_ref, bf16[512,768]{1,0:T(8,128)(2,1)S(1)} %bitcast.10, f32[512,512]{1,0:T(8,128)S(1)} %fusion.base_ref, f32[1,512]{1,0:T(1,128)S(1)} %bitcast.11), custom_call_target="tpu_custom_call" | custom-call | tf_op jit(solution)/shard_map/pallas_call | solution.py:276
  60.4 9.8 %all_to_all.21 = f32[16,1,128]{2,1,0:T(1,128)S(1)} all-to-all(f32[16,1,128]{2,1,0:T(1,128)S(1)} %get-tuple-element.7), channel_id=1, replica_groups=mesh['chrom'=32,'genome'=16] {'genome'}, dimensions={0} | all-to-all | bytes 16384 | tf_op jit(solution)/shard_map/all_to_all | solution.py:292
  70.2 20.4 %all_to_all.22 = f32[32,1,128]{2,1,0:T(1,128)S(1)} all-to-all(f32[32,1,128]{2,1,0:T(1,128)S(1)} %broadcast_in_dim.12), channel_id=1, replica_groups=mesh['chrom'=32,'genome'=16] {'chrom'}, dimensions={0} | all-to-all | bytes 32768 | tf_op jit(solution)/shard_map/all_to_all | solution.py:294
  90.6 0.1 reduce_sum.19
  90.6 0.5 bitcast_divide_fusion
  (2 shorter events, 0.0 us)
Async XLA Ops:
  33.8 3.6 %copy-start.1 = (bf16[768,512]{1,0:T(8,128)(2,1)S(1)}, bf16[768,512]{1,0:T(8,128)(2,1)}, u32[]{:S(2)}) copy-start(bf16[768,512]{1,0:T(8,128)(2,1)} %panel_hbm.1) | copy-start | bytes 2359300
  33.8 22.8 %all-to-all-start.1 = ((bf16[16,152,128]{2,1,0:T(8,128)(2,1)}), bf16[16,152,128]{2,1,0:T(8,128)(2,1)S(1)}, u32[]{:S(2)}, u32[]{:S(2)}) async-start(bf16[16,152,128]{2,1,0:T(8,128)(2,1)} %shard_map.60), calls=%async_computation.1 | async-start | bytes 1245184 | tf_op jit(solution)/shard_map/all_to_all | solution.py:269
  38.3 18.3 %copy-start = (f32[512]{0:T(512)S(1)}, f32[512]{0:T(512)}, u32[]{:S(2)}) copy-start(f32[512]{0:T(512)} %param.5) | copy-start | bytes 6148

commit v3 on v2

--- a/solution.py
+++ b/solution.py
@@ -45,7 +45,7 @@
     tiles = samples // TILE
     bands = tiles // 2
     arriving = []
-    for c in reversed(range(bands)):
+    for c in range(bands):
         band = pl.ds(2 * c * TILE, 2 * TILE)
         arriving.append(pltpu.make_async_copy(panel_hbm.at[band], panel_ref.at[band], sems.at[c]))
     small = [
@@ -62,8 +62,9 @@
         for row, owner, place, length in pieces(order[tile] * TILE, share):
             out_ref[owner, place : place + length, :] = value[row : row + length, :]
 
-    for c in reversed(range(bands)):
-        arriving[bands - 1 - c].wait()
+    for copy in arriving:
+        copy.wait()
+    for c in range(bands):
         low = 2 * c * TILE
         product = lax.dot_general(
             panel_ref[low:, :], panel_ref[low : low + 2 * TILE, :], NT, preferred_element_type=jnp.float32
@@ -235,6 +236,12 @@
     total_ref[...] = jnp.broadcast_to(jnp.sum(answer * answer, keepdims=True).reshape(1, 1, 1), total_ref.shape)
 
 
+def close_kernel(chroms, whitened_ref, group_ref, all_ref, out_ref, enrichment_ref):
+    out_ref[...] = whitened_ref[...]
+    overall = jnp.sum(all_ref[...], axis=0)
+    enrichment_ref[...] = group_ref[0] * chroms / overall
+
+
 def local(panel, zscores, block_chrom, lr_partner):
     samples, width = panel.shape
     owners = lax.axis_size("genome")
@@ -294,9 +301,17 @@
     of_all = lax.all_to_all(
         jnp.broadcast_to(group_sum, (chroms, 1, TILE)), "chrom", 0, 0, tiled=True
     )
-    group_sum, of_all = lax.optimization_barrier((group_sum, of_all))
-    enrichment = (group_sum * chroms / jnp.sum(of_all, axis=0, keepdims=True)).reshape(TILE)[:1]
-    return (whitened.reshape(width), enrichment)
+    whitened, enrichment = pl.pallas_call(
+        functools.partial(close_kernel, chroms),
+        out_shape=(
+            jax.ShapeDtypeStruct((1, width), jnp.float32),
+            jax.ShapeDtypeStruct((1, TILE), jnp.float32),
+        ),
+        in_specs=[VMEM] * 3,
+        out_specs=(VMEM, VMEM),
+        compiler_params=params,
+    )(whitened, group_sum, of_all)
+    return (whitened.reshape(width), enrichment.reshape(TILE)[:1])
 
 
 def solution(mesh):

time: 91.5 us -> 90.6 us (level)
  no operation moved by 1% of the time
where the time goes in v3:
time: 90.6 us; the launch traced here: 90.3 us
  blocking collectives  59.2 us (65%)
  waiting for transfers between devices  18.3 us (20%)
  Pallas kernels  6.92 us (8%)
  starting transfers between devices  3.62 us (4%)
  between operations  1.33 us (1%)
    all_to_all x1, blocking collectives, local(): held = lax.all_to_all(packed, 'genome', 0, 0, tiled=True)  29.1 us
    all_to_all x1, blocking collectives, local(): lax.all_to_all(jnp.broadcast_to(group_sum, (chroms, 1, TILE)), 'chrom', 0...  20.4 us
    all_to_all x1, waiting for transfers between devices, local(): sums = lax.all_to_all(mixed, 'genome', 0, 0, tiled=True)  18.3 us
    all_to_all x1, blocking collectives, local(): of_group = lax.all_to_all(totals, 'genome', 0, 0, tiled=True)  9.77 us
    all_to_all x1, starting transfers between devices, local(): sums = lax.all_to_all(mixed, 'genome', 0, 0, tiled=True)  3.62 us
    pallas_call x1, Pallas kernels, local(): pl.pallas_call(functools.partial(finish_kernel, share), out_shape=(jax.Sh...  3.3 us
  transfers between devices with their start and end apart: 1, of which 1 were waited for; matrix products, arithmetic and copies ran while one was open for 1% of the time, Pallas kernels for 0%

profile of v3, /device:TPU:1, one launch (start us, length us, event | category | flops | bytes accessed | tf_op | source)
XLA Modules:
  0.0 90.3 jit_solution(7125554215095868033)
XLA Ops:
  1.3 1.8 %shard_map.59 = bf16[16,152,128]{2,1,0:T(8,128)(2,1)S(1)} custom-call(s32[1,2]{1,0:T(1,128)} %partner_hbm.1, s32[1]{0:T(128)S(6)} %copy.7.chrom_ref, bf16[768,512]{1,0:T(8,128)(2,1)} %panel_hbm.1), custom_call_target="tpu_custom_call" | custom-call | tf_op jit(solution)/shard_map/pallas_call | solution.py:255
  3.1 29.1 %all_to_all.20.in_ref = bf16[16,152,128]{2,1,0:T(8,128)(2,1)S(1)} all-to-all(bf16[16,152,128]{2,1,0:T(8,128)(2,1)S(1)} %shard_map.59), channel_id=1, replica_groups=mesh['chrom'=32,'genome'=16] {'genome'}, dimensions={0} | all-to-all | bytes 1245184 | tf_op jit(solution)/shard_map/all_to_all | solution.py:267
  32.1 1.3 %shard_map.60 = bf16[16,152,128]{2,1,0:T(8,128)(2,1)} custom-call(bf16[16,152,128]{2,1,0:T(8,128)(2,1)S(1)} %all_to_all.20.in_ref), custom_call_target="tpu_custom_call" | custom-call | tf_op jit(solution)/shard_map/pallas_call | solution.py:269
  33.4 0.0 copy-start.1
  33.4 3.6 %all-to-all-start.1 = ((bf16[16,152,128]{2,1,0:T(8,128)(2,1)}), bf16[16,152,128]{2,1,0:T(8,128)(2,1)S(1)}, u32[]{:S(2)}, u32[]{:S(2)}) async-start(bf16[16,152,128]{2,1,0:T(8,128)(2,1)} %shard_map.60), calls=%async_computation.1 | async-start | bytes 1245184 | tf_op jit(solution)/shard_map/all_to_all | solution.py:276
  37.0 0.0 copy-done.1
  37.0 0.3 copy.6
  37.3 0.6 fusion.base_ref
  37.9 0.0 copy-start
  37.9 18.3 %all-to-all-done.1.sums_ref = bf16[16,152,128]{2,1,0:T(8,128)(2,1)S(1)} async-done(((bf16[16,152,128]{2,1,0:T(8,128)(2,1)}), bf16[16,152,128]{2,1,0:T(8,128)(2,1)S(1)}, u32[]{:S(2)}, u32[]{:S(2)}) %all-to-all-start.1) | async-done | bytes 622624 | tf_op jit(solution)/shard_map/all_to_all | solution.py:276
  56.2 0.0 copy-done
  56.2 3.3 %shard_map.61 = (f32[1,512]{1,0:T(1,128)S(1)}, f32[16,1,128]{2,1,0:T(1,128)S(1)}) custom-call(bf16[16,152,128]{2,1,0:T(8,128)(2,1)S(1)} %all-to-all-done.1.sums_ref, bf16[512,768]{1,0:T(8,128)(2,1)S(1)} %bitcast.8, f32[512,512]{1,0:T(8,128)S(1)} %fusion.base_ref, f32[1,512]{1,0:T(1,128)S(1)} %bitcast.10), custom_call_target="tpu_custom_call" | custom-call | tf_op jit(solution)/shard_map/pallas_call | solution.py:283
  59.5 9.8 %all_to_all.21 = f32[16,1,128]{2,1,0:T(1,128)S(1)} all-to-all(f32[16,1,128]{2,1,0:T(1,128)S(1)} %get-tuple-element.7), channel_id=1, replica_groups=mesh['chrom'=32,'genome'=16] {'genome'}, dimensions={0} | all-to-all | bytes 16384 | tf_op jit(solution)/shard_map/all_to_all | solution.py:299
  69.3 20.4 %all_to_all.22.all_ref = f32[32,1,128]{2,1,0:T(1,128)S(1)} all-to-all(f32[32,1,128]{2,1,0:T(1,128)S(1)} %broadcast_in_dim.9), channel_id=1, replica_groups=mesh['chrom'=32,'genome'=16] {'chrom'}, dimensions={0} | all-to-all | bytes 32768 | tf_op jit(solution)/shard_map/all_to_all | solution.py:301
  89.7 0.6 shard_map.62
  (2 shorter events, 0.0 us)
Async XLA Ops:
  33.4 3.6 %copy-start.1 = (bf16[768,512]{1,0:T(8,128)(2,1)S(1)}, bf16[768,512]{1,0:T(8,128)(2,1)}, u32[]{:S(2)}) copy-start(bf16[768,512]{1,0:T(8,128)(2,1)} %panel_hbm.1) | copy-start | bytes 2359300
  33.4 22.8 %all-to-all-start.1 = ((bf16[16,152,128]{2,1,0:T(8,128)(2,1)}), bf16[16,152,128]{2,1,0:T(8,128)(2,1)S(1)}, u32[]{:S(2)}, u32[]{:S(2)}) async-start(bf16[16,152,128]{2,1,0:T(8,128)(2,1)} %shard_map.60), calls=%async_computation.1 | async-start | bytes 1245184 | tf_op jit(solution)/shard_map/all_to_all | solution.py:276
  37.9 18.3 %copy-start = (f32[512]{0:T(512)S(1)}, f32[512]{0:T(512)}, u32[]{:S(2)}) copy-start(f32[512]{0:T(512)} %param.5) | copy-start | bytes 6148

commit v4 on v3

--- a/solution.py
+++ b/solution.py
@@ -141,9 +141,8 @@
     out_ref[:, share:, :] = mixed.reshape(owners, SUB, TILE)[:, :META, :].astype(jnp.bfloat16)
 
 
-def finish_kernel(share, sums_ref, columns_ref, base_ref, z_ref, out_ref, total_ref, half, scaled, first_iterate):
-    samples = columns_ref.shape[1]
-    width = columns_ref.shape[0]
+def finish_kernel(share, sums_ref, panel_ref, z_ref, out_ref, total_ref, half, scaled, first_iterate):
+    samples, width = panel_ref.shape
     tiles = samples // TILE
     order = {tile: n for n, tile in enumerate(tile_order(tiles))}
     rows, cols = grid_ids((TILE, TILE))
@@ -172,27 +171,23 @@
         place(2 * c + 1, 2 * c + 1, jnp.where(rows <= cols, packed, 0.0).astype(jnp.bfloat16))
         place(2 * c, 2 * c + 1, zero)
 
-    scale = leak_weight / (samples * samples)
-    columns = columns_ref[...]
     parts = []
     for c in range(tiles // 2):
-        top = (2 * c + 2) * TILE
+        low, top = 2 * c * TILE, (2 * c + 2) * TILE
         parts.append(
-            lax.dot_general(
-                columns[:, :top], half[2 * c * TILE : top, :top], NT, preferred_element_type=jnp.float32
-            )
-            * scale
-        )
-    turned = jnp.concatenate(parts, axis=1).astype(jnp.bfloat16)
-    matrix = (
-        base_ref[...]
-        + lax.dot_general(columns, turned, NT, preferred_element_type=jnp.float32)
-        + lax.dot_general(turned, columns, NT, preferred_element_type=jnp.float32)
-    )
-    norm = jnp.sqrt(jnp.sum(matrix * matrix, keepdims=True) + 1e-06)
-    matrix = matrix / norm
+            jnp.dot(half[low:top, :top], panel_ref[:top, :], preferred_element_type=jnp.float32)
+            * (leak_weight / samples)
+            + 0.5 * panel_ref[low:top, :].astype(jnp.float32)
+        )
+    weighted = jnp.concatenate(parts, axis=0).astype(jnp.bfloat16)
+    product = lax.dot_general(
+        panel_ref[...], weighted, (((0,), (0,)), ((), ())), preferred_element_type=jnp.float32
+    )
+    wide_rows, wide_cols = grid_ids((width, width))
+    matrix = product + product.T + jnp.where(wide_rows == wide_cols, ridge_term * samples, 0.0)
+    norm = jnp.sqrt(jnp.sum(matrix * matrix, keepdims=True) + 1e-06 * samples * samples)
+    matrix = matrix * (1.0 / norm)
     scaled[...] = matrix
-    wide_rows, wide_cols = grid_ids((width, width))
     first_iterate[...] = jnp.where(wide_rows == wide_cols, 1.5, 0.0) - 0.5 * matrix
 
     eye = rows == cols
@@ -275,18 +270,13 @@
     )(held)
     sums = lax.all_to_all(mixed, "genome", 0, 0, tiled=True)
 
-    columns = panel.T
-    base = lax.dot_general(
-        panel, panel, (((0,), (0,)), ((), ())), preferred_element_type=jnp.float32
-    ) * (1.0 / samples) + ridge_term * jnp.eye(width, dtype=jnp.float32)
-
     whitened, totals = pl.pallas_call(
         functools.partial(finish_kernel, share),
         out_shape=(
             jax.ShapeDtypeStruct((1, width), jnp.float32),
             jax.ShapeDtypeStruct((owners, 1, TILE), jnp.float32),
         ),
-        in_specs=[VMEM] * 4,
+        in_specs=[VMEM] * 3,
         out_specs=(VMEM, VMEM),
         scratch_shapes=[
             pltpu.VMEM((samples, samples), jnp.bfloat16),
@@ -294,7 +284,7 @@
             pltpu.VMEM((width, width), jnp.float32),
         ],
         compiler_params=params,
-    )(sums, columns, base, zscores.reshape(1, width))
+    )(sums, panel, zscores.reshape(1, width))
 
     of_group = lax.all_to_all(totals, "genome", 0, 0, tiled=True)
     group_sum = jnp.sum(of_group, axis=0, keepdims=True)

time: 90.6 us -> 88.6 us (0.978)
  blocking collectives: 59.2 us -> 81.2 us
  waiting for transfers between devices: 18.3 us -> 0 us
  starting transfers between devices: 3.62 us -> 0 us
  Pallas kernels: 6.92 us -> 5.81 us
    all_to_all x0 -> x1, blocking collectives: none -> 22.1 us  [local(): sums = lax.all_to_all(mixed, 'genome', 0, 0, tiled=True)]
    all_to_all x1 -> x0, waiting for transfers between devices: 18.3 us -> none  [local(): sums = lax.all_to_all(mixed, 'genome', 0, 0, tiled=True)]
    all_to_all x1 -> x0, starting transfers between devices: 3.62 us -> none  [local(): sums = lax.all_to_all(mixed, 'genome', 0, 0, tiled=True)]
  transfers between devices with their start and end apart: 1 -> 0, of which waited for: 1 -> 0; matrix products, arithmetic and copies ran while one was open for 1% -> 0% of each run, Pallas kernels for 0% -> 0%
where the time goes in v4:
time: 88.6 us; the launch traced here: 88.3 us
  blocking collectives  81.2 us (92%)
  Pallas kernels  5.81 us (7%)
  between operations  1.32 us (1%)
    all_to_all x1, blocking collectives, local(): held = lax.all_to_all(packed, 'genome', 0, 0, tiled=True)  29.1 us
    all_to_all x1, blocking collectives, local(): sums = lax.all_to_all(mixed, 'genome', 0, 0, tiled=True)  22.1 us
    all_to_all x1, blocking collectives, local(): lax.all_to_all(jnp.broadcast_to(group_sum, (chroms, 1, TILE)), 'chrom', 0...  20.4 us
    all_to_all x1, blocking collectives, local(): of_group = lax.all_to_all(totals, 'genome', 0, 0, tiled=True)  9.55 us
    pallas_call x1, Pallas kernels, local(): pl.pallas_call(functools.partial(finish_kernel, share), out_shape=(jax.Sh...  3.04 us
    pallas_call x1, Pallas kernels, local(): pl.pallas_call(functools.partial(gram_kernel, owners, share), out_shape=p...  1.77 us

profile of v4, /device:TPU:1, one launch (start us, length us, event | category | flops | bytes accessed | tf_op | source)
XLA Modules:
  0.0 88.3 jit_solution(11798723116877624829)
XLA Ops:
  1.3 1.8 %shard_map.59 = bf16[16,152,128]{2,1,0:T(8,128)(2,1)S(1)} custom-call(s32[1,2]{1,0:T(1,128)} %partner_hbm.1, s32[1]{0:T(128)S(6)} %copy.6.chrom_ref, bf16[768,512]{1,0:T(8,128)(2,1)} %panel_ref.1), custom_call_target="tpu_custom_call" | custom-call | tf_op jit(solution)/shard_map/pallas_call | solution.py:250
  3.1 29.1 %all_to_all.20.in_ref = bf16[16,152,128]{2,1,0:T(8,128)(2,1)S(1)} all-to-all(bf16[16,152,128]{2,1,0:T(8,128)(2,1)S(1)} %shard_map.59), channel_id=1, replica_groups=mesh['chrom'=32,'genome'=16] {'genome'}, dimensions={0} | all-to-all | bytes 1245184 | tf_op jit(solution)/shard_map/all_to_all | solution.py:262
  32.1 0.4 shard_map.60
  32.5 0.0 copy-start
  32.6 0.0 copy-start.1
  32.6 22.1 %all_to_all.21.sums_ref = bf16[16,152,128]{2,1,0:T(8,128)(2,1)S(1)} all-to-all(bf16[16,152,128]{2,1,0:T(8,128)(2,1)S(1)} %shard_map.60), channel_id=1, replica_groups=mesh['chrom'=32,'genome'=16] {'genome'}, dimensions={0} | all-to-all | bytes 1245184 | tf_op jit(solution)/shard_map/all_to_all | solution.py:271
  54.7 0.0 copy-done
  54.7 0.0 copy-done.1
  54.7 3.0 %shard_map.61 = (f32[1,512]{1,0:T(1,128)S(1)}, f32[16,1,128]{2,1,0:T(1,128)S(1)}) custom-call(bf16[16,152,128]{2,1,0:T(8,128)(2,1)S(1)} %all_to_all.21.sums_ref, bf16[768,512]{1,0:T(8,128)(2,1)S(1)} %copy-done, f32[1,512]{1,0:T(1,128)S(1)} %bitcast.6), custom_call_target="tpu_custom_call" | custom-call | tf_op jit(solution)/shard_map/pallas_call | solution.py:273
  57.7 9.5 %all_to_all.22 = f32[16,1,128]{2,1,0:T(1,128)S(1)} all-to-all(f32[16,1,128]{2,1,0:T(1,128)S(1)} %get-tuple-element.7), channel_id=1, replica_groups=mesh['chrom'=32,'genome'=16] {'genome'}, dimensions={0} | all-to-all | bytes 16384 | tf_op jit(solution)/shard_map/all_to_all | solution.py:289
  67.3 20.4 %all_to_all.23.all_ref = f32[32,1,128]{2,1,0:T(1,128)S(1)} all-to-all(f32[32,1,128]{2,1,0:T(1,128)S(1)} %broadcast_in_dim.9), channel_id=1, replica_groups=mesh['chrom'=32,'genome'=16] {'chrom'}, dimensions={0} | all-to-all | bytes 32768 | tf_op jit(solution)/shard_map/all_to_all | solution.py:291
  87.8 0.6 shard_map.62
  (2 shorter events, 0.0 us)
Async XLA Ops:
  32.5 22.2 %copy-start = (bf16[768,512]{1,0:T(8,128)(2,1)S(1)}, bf16[768,512]{1,0:T(8,128)(2,1)}, u32[]{:S(2)}) copy-start(bf16[768,512]{1,0:T(8,128)(2,1)} %panel_ref.1) | copy-start | bytes 2359300
  32.6 22.1 %copy-start.1 = (f32[512]{0:T(512)S(1)}, f32[512]{0:T(512)}, u32[]{:S(2)}) copy-start(f32[512]{0:T(512)} %param.5) | copy-start | bytes 6148

commit v5 on v4

--- a/solution.py
+++ b/solution.py
@@ -141,7 +141,7 @@
     out_ref[:, share:, :] = mixed.reshape(owners, SUB, TILE)[:, :META, :].astype(jnp.bfloat16)
 
 
-def finish_kernel(share, sums_ref, panel_ref, z_ref, out_ref, total_ref, half, scaled, first_iterate):
+def finish_kernel(share, sums_ref, panel_ref, z_ref, out_ref, total_ref, half, whole, shifted):
     samples, width = panel_ref.shape
     tiles = samples // TILE
     order = {tile: n for n, tile in enumerate(tile_order(tiles))}
@@ -183,15 +183,24 @@
     product = lax.dot_general(
         panel_ref[...], weighted, (((0,), (0,)), ((), ())), preferred_element_type=jnp.float32
     )
-    wide_rows, wide_cols = grid_ids((width, width))
-    matrix = product + product.T + jnp.where(wide_rows == wide_cols, ridge_term * samples, 0.0)
+    wide = width // TILE
+    eye = rows == cols
+    ridge = jnp.where(eye, ridge_term * samples, 0.0)
+    both = product + product.T
+
+    def with_ridge(m):
+        own, above = m * TILE, (m + 1) * TILE
+        band = both[own:above]
+        return jnp.concatenate([band[:, :own], band[:, own:above] + ridge, band[:, above:]][(m == 0):(2 if m == wide - 1 else 3)], axis=1)
+
+    matrix = jnp.concatenate([with_ridge(m) for m in range(wide)], axis=0)
+    whole[...] = matrix
+    shifted[...] = matrix
     norm = jnp.sqrt(jnp.sum(matrix * matrix, keepdims=True) + 1e-06 * samples * samples)
-    matrix = matrix * (1.0 / norm)
-    scaled[...] = matrix
-    first_iterate[...] = jnp.where(wide_rows == wide_cols, 1.5, 0.0) - 0.5 * matrix
-
-    eye = rows == cols
-    blocks = width // TILE
+    inverse = 1.0 / norm
+    for n in range(wide):
+        own = slice(n * TILE, (n + 1) * TILE)
+        shifted[own, own] = whole[own, own] - jnp.where(eye, 3.0 * norm, 0.0)
 
     def to_column(ref, row):
         return jnp.sum(ref[...] * row, axis=1, keepdims=True)
@@ -203,7 +212,7 @@
         return jnp.concatenate(
             [
                 jnp.sum(jnp.where(eye, column[n * TILE : (n + 1) * TILE], 0.0), axis=0, keepdims=True)
-                for n in range(blocks)
+                for n in range(wide)
             ],
             axis=1,
         )
@@ -212,20 +221,19 @@
         return jnp.concatenate(
             [
                 jnp.sum(jnp.where(eye, row[:, n * TILE : (n + 1) * TILE], 0.0), axis=1, keepdims=True)
-                for n in range(blocks)
+                for n in range(wide)
             ],
             axis=0,
         )
 
-    def second_iterate(column):
-        inner = to_row(scaled, column)
-        inner = to_column(first_iterate, inner)
-        inner = to_row(first_iterate, inner)
-        return 0.5 * to_column(first_iterate, 3.0 * turned_column(column) - inner)
+    def second_iterate(column, factor):
+        inner = to_row(whole, column) * inverse
+        inner = to_row(shifted, to_column(shifted, inner)) * (0.25 * inverse * inverse)
+        return to_column(shifted, (3.0 * turned_column(column) - inner) * ((-0.25 * factor) * inverse))
 
     z_row = z_ref[...]
-    product = second_iterate(second_iterate(to_column(scaled, z_row)))
-    answer = 0.5 * second_iterate(3.0 * turned_row(z_row) - product)
+    product = second_iterate(second_iterate(to_column(whole, z_row * inverse), 1.0), 1.0)
+    answer = second_iterate(3.0 * turned_row(z_row) - product, 0.5)
     answer = turned_column(answer)
     out_ref[...] = answer
     total_ref[...] = jnp.broadcast_to(jnp.sum(answer * answer, keepdims=True).reshape(1, 1, 1), total_ref.shape)

time: 88.6 us -> 88.5 us (level)
  no operation moved by 1% of the time
where the time goes in v5:
time: 88.5 us; the launch traced here: 88.2 us
  blocking collectives  81.2 us (92%)
  Pallas kernels  5.68 us (6%)
  between operations  1.32 us (1%)
    all_to_all x1, blocking collectives, local(): held = lax.all_to_all(packed, 'genome', 0, 0, tiled=True)  29.1 us
    all_to_all x1, blocking collectives, local(): sums = lax.all_to_all(mixed, 'genome', 0, 0, tiled=True)  22.1 us
    all_to_all x1, blocking collectives, local(): lax.all_to_all(jnp.broadcast_to(group_sum, (chroms, 1, TILE)), 'chrom', 0...  20.4 us
    all_to_all x1, blocking collectives, local(): of_group = lax.all_to_all(totals, 'genome', 0, 0, tiled=True)  9.55 us
    pallas_call x1, Pallas kernels, local(): pl.pallas_call(functools.partial(finish_kernel, share), out_shape=(jax.Sh...  2.91 us
    pallas_call x1, Pallas kernels, local(): pl.pallas_call(functools.partial(gram_kernel, owners, share), out_shape=p...  1.77 us

profile of v5, /device:TPU:1, one launch (start us, length us, event | category | flops | bytes accessed | tf_op | source)
XLA Modules:
  0.0 88.2 jit_solution(8520539757755448641)
XLA Ops:
  1.3 1.8 %shard_map.59 = bf16[16,152,128]{2,1,0:T(8,128)(2,1)S(1)} custom-call(s32[1,2]{1,0:T(1,128)} %partner_hbm.1, s32[1]{0:T(128)S(6)} %copy.6.chrom_ref, bf16[768,512]{1,0:T(8,128)(2,1)} %panel_ref.1), custom_call_target="tpu_custom_call" | custom-call | tf_op jit(solution)/shard_map/pallas_call | solution.py:258
  3.1 29.1 %all_to_all.20.in_ref = bf16[16,152,128]{2,1,0:T(8,128)(2,1)S(1)} all-to-all(bf16[16,152,128]{2,1,0:T(8,128)(2,1)S(1)} %shard_map.59), channel_id=1, replica_groups=mesh['chrom'=32,'genome'=16] {'genome'}, dimensions={0} | all-to-all | bytes 1245184 | tf_op jit(solution)/shard_map/all_to_all | solution.py:270
  32.1 0.4 shard_map.60
  32.5 0.0 copy-start
  32.6 0.0 copy-start.1
  32.6 22.1 %all_to_all.21.sums_ref = bf16[16,152,128]{2,1,0:T(8,128)(2,1)S(1)} all-to-all(bf16[16,152,128]{2,1,0:T(8,128)(2,1)S(1)} %shard_map.60), channel_id=1, replica_groups=mesh['chrom'=32,'genome'=16] {'genome'}, dimensions={0} | all-to-all | bytes 1245184 | tf_op jit(solution)/shard_map/all_to_all | solution.py:279
  54.7 0.0 copy-done
  54.7 0.0 copy-done.1
  54.7 2.9 %shard_map.61 = (f32[1,512]{1,0:T(1,128)S(1)}, f32[16,1,128]{2,1,0:T(1,128)S(1)}) custom-call(bf16[16,152,128]{2,1,0:T(8,128)(2,1)S(1)} %all_to_all.21.sums_ref, bf16[768,512]{1,0:T(8,128)(2,1)S(1)} %copy-done, f32[1,512]{1,0:T(1,128)S(1)} %bitcast.6), custom_call_target="tpu_custom_call" | custom-call | tf_op jit(solution)/shard_map/pallas_call | solution.py:281
  57.6 9.6 %all_to_all.22 = f32[16,1,128]{2,1,0:T(1,128)S(1)} all-to-all(f32[16,1,128]{2,1,0:T(1,128)S(1)} %get-tuple-element.7), channel_id=1, replica_groups=mesh['chrom'=32,'genome'=16] {'genome'}, dimensions={0} | all-to-all | bytes 16384 | tf_op jit(solution)/shard_map/all_to_all | solution.py:297
  67.2 20.4 %all_to_all.23.all_ref = f32[32,1,128]{2,1,0:T(1,128)S(1)} all-to-all(f32[32,1,128]{2,1,0:T(1,128)S(1)} %broadcast_in_dim.9), channel_id=1, replica_groups=mesh['chrom'=32,'genome'=16] {'chrom'}, dimensions={0} | all-to-all | bytes 32768 | tf_op jit(solution)/shard_map/all_to_all | solution.py:299
  87.6 0.6 shard_map.62
  (2 shorter events, 0.0 us)
Async XLA Ops:
  32.5 22.2 %copy-start = (bf16[768,512]{1,0:T(8,128)(2,1)S(1)}, bf16[768,512]{1,0:T(8,128)(2,1)}, u32[]{:S(2)}) copy-start(bf16[768,512]{1,0:T(8,128)(2,1)} %panel_ref.1) | copy-start | bytes 2359300
  32.6 22.1 %copy-start.1 = (f32[512]{0:T(512)S(1)}, f32[512]{0:T(512)}, u32[]{:S(2)}) copy-start(f32[512]{0:T(512)} %param.5) | copy-start | bytes 6148

commit v6 on v5

--- a/solution.py
+++ b/solution.py
@@ -96,7 +96,7 @@
         out_ref[owner, share : share + META, :] = meta
 
 
-def mix_kernel(in_ref, out_ref):
+def mix_kernel(in_ref, out_ref, diagonal_ref):
     owners, height, _ = in_ref.shape
     share = height - META
     meta = in_ref[:, share:, :].astype(jnp.float32)
@@ -138,10 +138,12 @@
     mixed = jnp.dot(
         weights, padded.reshape(owners * SUB, TILE).astype(jnp.bfloat16), preferred_element_type=jnp.float32
     )
-    out_ref[:, share:, :] = mixed.reshape(owners, SUB, TILE)[:, :META, :].astype(jnp.bfloat16)
-
-
-def finish_kernel(share, sums_ref, panel_ref, z_ref, out_ref, total_ref, half, whole, shifted):
+    diagonal_ref[...] = mixed.reshape(owners, SUB, TILE)[:, :META, :]
+
+
+def finish_kernel(share, sums_ref, diagonal_ref, panel_ref, z_hbm, out_ref, total_ref, half, whole, shifted, z_ref, sem):
+    arriving = pltpu.make_async_copy(z_hbm, z_ref, sem)
+    arriving.start()
     samples, width = panel_ref.shape
     tiles = samples // TILE
     order = {tile: n for n, tile in enumerate(tile_order(tiles))}
@@ -160,7 +162,7 @@
     def place(i, j, value):
         half[i * TILE : (i + 1) * TILE, j * TILE : (j + 1) * TILE] = value
 
-    meta = sums_ref[0, share : share + META, :].astype(jnp.float32)
+    meta = diagonal_ref[lax.axis_index("genome")]
     for c in range(tiles // 2):
         for j in (2 * c, 2 * c + 1):
             for i in range(j + 1, tiles):
@@ -231,6 +233,7 @@
         inner = to_row(shifted, to_column(shifted, inner)) * (0.25 * inverse * inverse)
         return to_column(shifted, (3.0 * turned_column(column) - inner) * ((-0.25 * factor) * inverse))
 
+    arriving.wait()
     z_row = z_ref[...]
     product = second_iterate(second_iterate(to_column(whole, z_row * inverse), 1.0), 1.0)
     answer = second_iterate(3.0 * turned_row(z_row) - product, 0.5)
@@ -269,11 +272,14 @@
     )(lr_hbm, block_chrom, panel_hbm)
     held = lax.all_to_all(packed, "genome", 0, 0, tiled=True)
 
-    mixed = pl.pallas_call(
+    mixed, diagonals = pl.pallas_call(
         mix_kernel,
-        out_shape=packed_shape,
+        out_shape=(
+            jax.ShapeDtypeStruct((owners, share, TILE), jnp.bfloat16),
+            jax.ShapeDtypeStruct((owners, META, TILE), jnp.float32),
+        ),
         in_specs=[VMEM],
-        out_specs=VMEM,
+        out_specs=(VMEM, VMEM),
         compiler_params=params,
     )(held)
     sums = lax.all_to_all(mixed, "genome", 0, 0, tiled=True)
@@ -284,15 +290,17 @@
             jax.ShapeDtypeStruct((1, width), jnp.float32),
             jax.ShapeDtypeStruct((owners, 1, TILE), jnp.float32),
         ),
-        in_specs=[VMEM] * 3,
+        in_specs=[VMEM, VMEM, VMEM, HBM],
         out_specs=(VMEM, VMEM),
         scratch_shapes=[
             pltpu.VMEM((samples, samples), jnp.bfloat16),
             pltpu.VMEM((width, width), jnp.float32),
             pltpu.VMEM((width, width), jnp.float32),
+            pltpu.VMEM((1, width), jnp.float32),
+            pltpu.SemaphoreType.DMA,
         ],
         compiler_params=params,
-    )(sums, panel, zscores.reshape(1, width))
+    )(sums, diagonals, panel, pltpu.with_memory_space_constraint(zscores.reshape(1, width), pltpu.HBM))
 
     of_group = lax.all_to_all(totals, "genome", 0, 0, tiled=True)
     group_sum = jnp.sum(of_group, axis=0, keepdims=True)

time: 88.5 us -> 87.8 us (level)
  no operation moved by 1% of the time
where the time goes in v6:
time: 87.8 us; the launch traced here: 87.5 us
  blocking collectives  80.5 us (92%)
  Pallas kernels  5.73 us (7%)
  between operations  1.3 us (1%)
    all_to_all x1, blocking collectives, local(): held = lax.all_to_all(packed, 'genome', 0, 0, tiled=True)  29.1 us
    all_to_all x1, blocking collectives, local(): sums = lax.all_to_all(mixed, 'genome', 0, 0, tiled=True)  21.4 us
    all_to_all x1, blocking collectives, local(): lax.all_to_all(jnp.broadcast_to(group_sum, (chroms, 1, TILE)), 'chrom', 0...  20.4 us
    all_to_all x1, blocking collectives, local(): of_group = lax.all_to_all(totals, 'genome', 0, 0, tiled=True)  9.63 us
    pallas_call x1, Pallas kernels, local(): pl.pallas_call(functools.partial(finish_kernel, share), out_shape=(jax.Sh...  2.95 us
    pallas_call x1, Pallas kernels, local(): pl.pallas_call(functools.partial(gram_kernel, owners, share), out_shape=p...  1.77 us

profile of v6, /device:TPU:1, one launch (start us, length us, event | category | flops | bytes accessed | tf_op | source)
XLA Modules:
  0.0 87.5 jit_solution(4664018934621203152)
XLA Ops:
  1.3 1.8 %shard_map.59 = bf16[16,152,128]{2,1,0:T(8,128)(2,1)S(1)} custom-call(s32[1,2]{1,0:T(1,128)} %partner_hbm.1, s32[1]{0:T(128)S(6)} %copy.6.chrom_ref, bf16[768,512]{1,0:T(8,128)(2,1)} %panel_ref.1), custom_call_target="tpu_custom_call" | custom-call | tf_op jit(solution)/shard_map/pallas_call | solution.py:261
  3.1 29.1 %all_to_all.20.in_ref = bf16[16,152,128]{2,1,0:T(8,128)(2,1)S(1)} all-to-all(bf16[16,152,128]{2,1,0:T(8,128)(2,1)S(1)} %shard_map.59), channel_id=1, replica_groups=mesh['chrom'=32,'genome'=16] {'genome'}, dimensions={0} | all-to-all | bytes 1245184 | tf_op jit(solution)/shard_map/all_to_all | solution.py:273
  32.1 0.0 copy-start
  32.1 0.4 shard_map.60
  32.5 21.4 %all_to_all.21.sums_ref = bf16[16,144,128]{2,1,0:T(8,128)(2,1)S(1)} all-to-all(bf16[16,144,128]{2,1,0:T(8,128)(2,1)S(1)} %get-tuple-element.8), channel_id=1, replica_groups=mesh['chrom'=32,'genome'=16] {'genome'}, dimensions={0} | all-to-all | bytes 1179648 | tf_op jit(solution)/shard_map/all_to_all | solution.py:285
  53.9 0.0 copy-done
  53.9 3.0 %shard_map.61 = (f32[1,512]{1,0:T(1,128)S(1)}, f32[16,1,128]{2,1,0:T(1,128)S(1)}) custom-call(bf16[16,144,128]{2,1,0:T(8,128)(2,1)S(1)} %all_to_all.21.sums_ref, f32[16,8,128]{2,1,0:T(8,128)S(1)} %get-tuple-element.9.diagonal_ref, bf16[768,512]{1,0:T(8,128)(2,1)S(1)} %copy-done, f32[1,512]{1,0:T(1,128)} %bitcast.6), custom_call_target="tpu_custom_call" | custom-call | tf_op jit(solution)/shard_map/pallas_call | solution.py:287
  56.9 9.6 %all_to_all.22 = f32[16,1,128]{2,1,0:T(1,128)S(1)} all-to-all(f32[16,1,128]{2,1,0:T(1,128)S(1)} %get-tuple-element.11), channel_id=1, replica_groups=mesh['chrom'=32,'genome'=16] {'genome'}, dimensions={0} | all-to-all | bytes 16384 | tf_op jit(solution)/shard_map/all_to_all | solution.py:305
  66.5 20.4 %all_to_all.23.all_ref = f32[32,1,128]{2,1,0:T(1,128)S(1)} all-to-all(f32[32,1,128]{2,1,0:T(1,128)S(1)} %broadcast_in_dim.9), channel_id=1, replica_groups=mesh['chrom'=32,'genome'=16] {'chrom'}, dimensions={0} | all-to-all | bytes 32768 | tf_op jit(solution)/shard_map/all_to_all | solution.py:307
  87.0 0.6 shard_map.62
  (2 shorter events, 0.0 us)
Async XLA Ops:
  32.1 21.8 %copy-start = (bf16[768,512]{1,0:T(8,128)(2,1)S(1)}, bf16[768,512]{1,0:T(8,128)(2,1)}, u32[]{:S(2)}) copy-start(bf16[768,512]{1,0:T(8,128)(2,1)} %panel_ref.1) | copy-start | bytes 2359300

commit v7 on v6

--- a/solution.py
+++ b/solution.py
@@ -40,7 +40,7 @@
     return out
 
 
-def gram_kernel(owners, share, partner_hbm, chrom_ref, panel_hbm, out_ref, panel_ref, partner_ref, sems):
+def gram_kernel(owners, share, partner_hbm, chrom_ref, panel_hbm, z_hbm, out_ref, z_ref, panel_ref, partner_ref, sems):
     samples = panel_ref.shape[0]
     tiles = samples // TILE
     bands = tiles // 2
@@ -50,6 +50,7 @@
         arriving.append(pltpu.make_async_copy(panel_hbm.at[band], panel_ref.at[band], sems.at[c]))
     small = [
         pltpu.make_async_copy(partner_hbm, partner_ref, sems.at[bands]),
+        pltpu.make_async_copy(z_hbm, z_ref, sems.at[bands + 1]),
     ]
     for copy in arriving + small:
         copy.start()
@@ -141,9 +142,7 @@
     diagonal_ref[...] = mixed.reshape(owners, SUB, TILE)[:, :META, :]
 
 
-def finish_kernel(share, sums_ref, diagonal_ref, panel_ref, z_hbm, out_ref, total_ref, half, whole, shifted, z_ref, sem):
-    arriving = pltpu.make_async_copy(z_hbm, z_ref, sem)
-    arriving.start()
+def finish_kernel(share, sums_ref, diagonal_ref, panel_ref, z_ref, out_ref, total_ref, half, whole, shifted):
     samples, width = panel_ref.shape
     tiles = samples // TILE
     order = {tile: n for n, tile in enumerate(tile_order(tiles))}
@@ -233,7 +232,6 @@
         inner = to_row(shifted, to_column(shifted, inner)) * (0.25 * inverse * inverse)
         return to_column(shifted, (3.0 * turned_column(column) - inner) * ((-0.25 * factor) * inverse))
 
-    arriving.wait()
     z_row = z_ref[...]
     product = second_iterate(second_iterate(to_column(whole, z_row * inverse), 1.0), 1.0)
     answer = second_iterate(3.0 * turned_row(z_row) - product, 0.5)
@@ -257,19 +255,21 @@
     packed_shape = jax.ShapeDtypeStruct((owners, share + META, TILE), jnp.bfloat16)
     params = pltpu.CompilerParams(vmem_limit_bytes=48 * 2**20)
 
-    lr_hbm, panel_hbm = (pltpu.with_memory_space_constraint(x, pltpu.HBM) for x in (lr_partner, panel))
-    packed = pl.pallas_call(
+    lr_hbm, panel_hbm, z_hbm = (
+        pltpu.with_memory_space_constraint(x, pltpu.HBM) for x in (lr_partner, panel, zscores.reshape(1, width))
+    )
+    packed, scores = pl.pallas_call(
         functools.partial(gram_kernel, owners, share),
-        out_shape=packed_shape,
-        in_specs=[HBM, SMEM, HBM],
-        out_specs=VMEM,
+        out_shape=(packed_shape, jax.ShapeDtypeStruct((1, width), jnp.float32)),
+        in_specs=[HBM, SMEM, HBM, HBM],
+        out_specs=(VMEM, VMEM),
         scratch_shapes=[
             pltpu.VMEM(panel.shape, panel.dtype),
             pltpu.SMEM(lr_partner.shape, jnp.int32),
-            pltpu.SemaphoreType.DMA((tiles // 2 + 1,)),
+            pltpu.SemaphoreType.DMA((tiles // 2 + 2,)),
         ],
         compiler_params=params,
-    )(lr_hbm, block_chrom, panel_hbm)
+    )(lr_hbm, block_chrom, panel_hbm, z_hbm)
     held = lax.all_to_all(packed, "genome", 0, 0, tiled=True)
 
     mixed, diagonals = pl.pallas_call(
@@ -290,17 +290,15 @@
             jax.ShapeDtypeStruct((1, width), jnp.float32),
             jax.ShapeDtypeStruct((owners, 1, TILE), jnp.float32),
         ),
-        in_specs=[VMEM, VMEM, VMEM, HBM],
+        in_specs=[VMEM] * 4,
         out_specs=(VMEM, VMEM),
         scratch_shapes=[
             pltpu.VMEM((samples, samples), jnp.bfloat16),
             pltpu.VMEM((width, width), jnp.float32),
             pltpu.VMEM((width, width), jnp.float32),
-            pltpu.VMEM((1, width), jnp.float32),
-            pltpu.SemaphoreType.DMA,
         ],
         compiler_params=params,
-    )(sums, diagonals, panel, pltpu.with_memory_space_constraint(zscores.reshape(1, width), pltpu.HBM))
+    )(sums, diagonals, panel, scores)
 
     of_group = lax.all_to_all(totals, "genome", 0, 0, tiled=True)
     group_sum = jnp.sum(of_group, axis=0, keepdims=True)

time: 87.8 us -> 87.8 us (level)
  no operation moved by 1% of the time
where the time goes in v7:
time: 87.8 us; the launch traced here: 87.5 us
  blocking collectives  80.5 us (92%)
  Pallas kernels  5.7 us (6%)
  between operations  1.3 us (1%)
    all_to_all x1, blocking collectives, local(): held = lax.all_to_all(packed, 'genome', 0, 0, tiled=True)  29 us
    all_to_all x1, blocking collectives, local(): sums = lax.all_to_all(mixed, 'genome', 0, 0, tiled=True)  21.4 us
    all_to_all x1, blocking collectives, local(): lax.all_to_all(jnp.broadcast_to(group_sum, (chroms, 1, TILE)), 'chrom', 0...  20.4 us
    all_to_all x1, blocking collectives, local(): of_group = lax.all_to_all(totals, 'genome', 0, 0, tiled=True)  9.63 us
    pallas_call x1, Pallas kernels, local(): pl.pallas_call(functools.partial(finish_kernel, share), out_shape=(jax.Sh...  2.92 us
    pallas_call x1, Pallas kernels, local(): pl.pallas_call(functools.partial(gram_kernel, owners, share), out_shape=(...  1.78 us

profile of v7, /device:TPU:1, one launch (start us, length us, event | category | flops | bytes accessed | tf_op | source)
XLA Modules:
  0.0 87.5 jit_solution(6593109043451692607)
XLA Ops:
  1.3 1.8 %shard_map.59 = (bf16[16,152,128]{2,1,0:T(8,128)(2,1)S(1)}, f32[1,512]{1,0:T(1,128)S(1)}) custom-call(s32[1,2]{1,0:T(1,128)} %partner_hbm.1, s32[1]{0:T(128)S(6)} %copy.6.chrom_ref, bf16[768,512]{1,0:T(8,128)(2,1)} %panel_ref.1, f32[1,512]{1,0:T(1,128)} %bitcast.6), custom_call_target="tpu_custom_call" | custom-call | tf_op jit(solution)/shard_map/pallas_call | solution.py:261
  3.1 29.0 %all_to_all.20.in_ref = bf16[16,152,128]{2,1,0:T(8,128)(2,1)S(1)} all-to-all(bf16[16,152,128]{2,1,0:T(8,128)(2,1)S(1)} %get-tuple-element.10), channel_id=1, replica_groups=mesh['chrom'=32,'genome'=16] {'genome'}, dimensions={0} | all-to-all | bytes 1245184 | tf_op jit(solution)/shard_map/all_to_all | solution.py:273
  32.1 0.0 copy-start
  32.1 0.4 shard_map.60
  32.5 21.4 %all_to_all.21.sums_ref = bf16[16,144,128]{2,1,0:T(8,128)(2,1)S(1)} all-to-all(bf16[16,144,128]{2,1,0:T(8,128)(2,1)S(1)} %get-tuple-element.11), channel_id=1, replica_groups=mesh['chrom'=32,'genome'=16] {'genome'}, dimensions={0} | all-to-all | bytes 1179648 | tf_op jit(solution)/shard_map/all_to_all | solution.py:285
  53.9 0.0 copy-done
  53.9 2.9 %shard_map.61 = (f32[1,512]{1,0:T(1,128)S(1)}, f32[16,1,128]{2,1,0:T(1,128)S(1)}) custom-call(bf16[16,144,128]{2,1,0:T(8,128)(2,1)S(1)} %all_to_all.21.sums_ref, f32[16,8,128]{2,1,0:T(8,128)S(1)} %get-tuple-element.12.diagonal_ref, bf16[768,512]{1,0:T(8,128)(2,1)S(1)} %copy-done, f32[1,512]{1,0:T(1,128)S(1)} %get-tuple-element.13.z_ref), custom_call_target="tpu_custom_call" | custom-call | tf_op jit(solution)/shard_map/pallas_call | solution.py:287
  56.8 9.6 %all_to_all.22 = f32[16,1,128]{2,1,0:T(1,128)S(1)} all-to-all(f32[16,1,128]{2,1,0:T(1,128)S(1)} %get-tuple-element.15), channel_id=1, replica_groups=mesh['chrom'=32,'genome'=16] {'genome'}, dimensions={0} | all-to-all | bytes 16384 | tf_op jit(solution)/shard_map/all_to_all | solution.py:303
  66.5 20.4 %all_to_all.23.all_ref = f32[32,1,128]{2,1,0:T(1,128)S(1)} all-to-all(f32[32,1,128]{2,1,0:T(1,128)S(1)} %broadcast_in_dim.9), channel_id=1, replica_groups=mesh['chrom'=32,'genome'=16] {'chrom'}, dimensions={0} | all-to-all | bytes 32768 | tf_op jit(solution)/shard_map/all_to_all | solution.py:305
  86.9 0.6 shard_map.62
  (2 shorter events, 0.0 us)
Async XLA Ops:
  32.1 21.8 %copy-start = (bf16[768,512]{1,0:T(8,128)(2,1)S(1)}, bf16[768,512]{1,0:T(8,128)(2,1)}, u32[]{:S(2)}) copy-start(bf16[768,512]{1,0:T(8,128)(2,1)} %panel_ref.1) | copy-start | bytes 2359300

commit v8 on v6

--- a/solution.py
+++ b/solution.py
@@ -182,8 +182,14 @@
             + 0.5 * panel_ref[low:top, :].astype(jnp.float32)
         )
     weighted = jnp.concatenate(parts, axis=0).astype(jnp.bfloat16)
-    product = lax.dot_general(
-        panel_ref[...], weighted, (((0,), (0,)), ((), ())), preferred_element_type=jnp.float32
+    product = jnp.concatenate(
+        [
+            lax.dot_general(
+                panel_ref[:, k : k + 2 * TILE], weighted, (((0,), (0,)), ((), ())), preferred_element_type=jnp.float32
+            )
+            for k in range(0, width, 2 * TILE)
+        ],
+        axis=0,
     )
     wide = width // TILE
     eye = rows == cols

time: 87.8 us -> 87.8 us (level)
  no operation moved by 1% of the time
where the time goes in v8:
time: 87.8 us; the launch traced here: 87.6 us
  blocking collectives  80.5 us (92%)
  Pallas kernels  5.73 us (7%)
  between operations  1.3 us (1%)
    all_to_all x1, blocking collectives, local(): held = lax.all_to_all(packed, 'genome', 0, 0, tiled=True)  29.1 us
    all_to_all x1, blocking collectives, local(): sums = lax.all_to_all(mixed, 'genome', 0, 0, tiled=True)  21.4 us
    all_to_all x1, blocking collectives, local(): lax.all_to_all(jnp.broadcast_to(group_sum, (chroms, 1, TILE)), 'chrom', 0...  20.4 us
    all_to_all x1, blocking collectives, local(): of_group = lax.all_to_all(totals, 'genome', 0, 0, tiled=True)  9.63 us
    pallas_call x1, Pallas kernels, local(): pl.pallas_call(functools.partial(finish_kernel, share), out_shape=(jax.Sh...  2.96 us
    pallas_call x1, Pallas kernels, local(): pl.pallas_call(functools.partial(gram_kernel, owners, share), out_shape=p...  1.77 us

profile of v8, /device:TPU:1, one launch (start us, length us, event | category | flops | bytes accessed | tf_op | source)
XLA Modules:
  0.0 87.6 jit_solution(955367878031541590)
XLA Ops:
  1.3 1.8 %shard_map.59 = bf16[16,152,128]{2,1,0:T(8,128)(2,1)S(1)} custom-call(s32[1,2]{1,0:T(1,128)} %partner_hbm.1, s32[1]{0:T(128)S(6)} %copy.6.chrom_ref, bf16[768,512]{1,0:T(8,128)(2,1)} %panel_ref.1), custom_call_target="tpu_custom_call" | custom-call | tf_op jit(solution)/shard_map/pallas_call | solution.py:267
  3.1 29.1 %all_to_all.20.in_ref = bf16[16,152,128]{2,1,0:T(8,128)(2,1)S(1)} all-to-all(bf16[16,152,128]{2,1,0:T(8,128)(2,1)S(1)} %shard_map.59), channel_id=1, replica_groups=mesh['chrom'=32,'genome'=16] {'genome'}, dimensions={0} | all-to-all | bytes 1245184 | tf_op jit(solution)/shard_map/all_to_all | solution.py:279
  32.1 0.0 copy-start
  32.1 0.4 shard_map.60
  32.5 21.4 %all_to_all.21.sums_ref = bf16[16,144,128]{2,1,0:T(8,128)(2,1)S(1)} all-to-all(bf16[16,144,128]{2,1,0:T(8,128)(2,1)S(1)} %get-tuple-element.8), channel_id=1, replica_groups=mesh['chrom'=32,'genome'=16] {'genome'}, dimensions={0} | all-to-all | bytes 1179648 | tf_op jit(solution)/shard_map/all_to_all | solution.py:291
  53.9 0.0 copy-done
  53.9 3.0 %shard_map.61 = (f32[1,512]{1,0:T(1,128)S(1)}, f32[16,1,128]{2,1,0:T(1,128)S(1)}) custom-call(bf16[16,144,128]{2,1,0:T(8,128)(2,1)S(1)} %all_to_all.21.sums_ref, f32[16,8,128]{2,1,0:T(8,128)S(1)} %get-tuple-element.9.diagonal_ref, bf16[768,512]{1,0:T(8,128)(2,1)S(1)} %copy-done, f32[1,512]{1,0:T(1,128)} %bitcast.6), custom_call_target="tpu_custom_call" | custom-call | tf_op jit(solution)/shard_map/pallas_call | solution.py:293
  56.9 9.6 %all_to_all.22 = f32[16,1,128]{2,1,0:T(1,128)S(1)} all-to-all(f32[16,1,128]{2,1,0:T(1,128)S(1)} %get-tuple-element.11), channel_id=1, replica_groups=mesh['chrom'=32,'genome'=16] {'genome'}, dimensions={0} | all-to-all | bytes 16384 | tf_op jit(solution)/shard_map/all_to_all | solution.py:311
  66.5 20.4 %all_to_all.23.all_ref = f32[32,1,128]{2,1,0:T(1,128)S(1)} all-to-all(f32[32,1,128]{2,1,0:T(1,128)S(1)} %broadcast_in_dim.9), channel_id=1, replica_groups=mesh['chrom'=32,'genome'=16] {'chrom'}, dimensions={0} | all-to-all | bytes 32768 | tf_op jit(solution)/shard_map/all_to_all | solution.py:313
  87.0 0.6 shard_map.62
  (2 shorter events, 0.0 us)
Async XLA Ops:
  32.1 21.8 %copy-start = (bf16[768,512]{1,0:T(8,128)(2,1)S(1)}, bf16[768,512]{1,0:T(8,128)(2,1)}, u32[]{:S(2)}) copy-start(bf16[768,512]{1,0:T(8,128)(2,1)} %panel_ref.1) | copy-start | bytes 2359300
